TPU v7x, 256 devices: a whole 4x4x8 slice. The times are simulated.
256 devices in a mesh: space: 16 (over y_hi, x, core), batch: 16 (over z, y_lo).
Axes of the slice: x: 4, y: 4 (y_hi: 2, y_lo: 2; y = y_hi * 2 + y_lo), z: 8, core: 2. Of those that a mesh axis runs over, the one named last changes fastest.
Arguments:
- inputs: bfloat16 [16, 112, 7, 7, 1024], P('batch', 'space'), may hold values from -60 to 60
- grad_out: bfloat16 [16, 112, 7, 7, 1024], P('batch', 'space'), may hold values from -6 to 6
- fluid: int32 [112, 7, 7], P('space'), may hold values 0 or 1
- w_qkv: bfloat16 [1024, 3072], P('batch')
- qkv_bias: float32 [3072], replicated, may hold values from -3 to 3
- w_proj: bfloat16 [1024, 1024], P('batch'), may hold values from -0.1875 to 0.1875
- ln_gain: float32 [1024], replicated, may hold values from 0.5 to 1.5
Outputs:
- grad_input: bfloat16 [16, 112, 7, 7, 1024], P('batch', 'space')
- grad_qkv: float32 [1024, 3072], P('batch')
- grad_proj: float32 [1024, 1024], P('batch')
- grad_gain: float32 [1024], replicated
- grad_bias: float32 [3072], replicated
All inputs are finite; a program needn't handle non-finite values. No bound on the sum of `fluid` on one device may be relied on, other than what follows from the above.
Results may differ from a plain program's by a relative error of at most 0.03.
Values may be sent and summed in bfloat16 or wider, within the bound.
No kernel may reach another device: no remote copies, remote signals or barrier semaphores. Data moves between devices by JAX's collectives and lax.ppermute only.
A program may use at most 128 MiB of HBM per device.

v0:
```python
import itertools
import math

import jax
import jax.numpy as jnp
from jax import lax
from jax.experimental import pallas as pl
from jax.experimental.pallas import tpu as pltpu
from jax.sharding import PartitionSpec as P

HEADS = 16
WIN = 7
SHIFT = 3
TOKENS = WIN**3
ROWS = 352
EPS = 1e-05
NEG = -1e30
BOTH = ("space", "batch")


def flat(x, y, z, c):
    return ((y // 2 * 4 + x) * 2 + c) * 16 + z * 2 + y % 2


def places():
    s = lax.axis_index("space").astype(jnp.uint32)
    b = lax.axis_index("batch").astype(jnp.uint32)
    return (s >> 1) & 3, (s >> 3) * 2 + (b & 1), b >> 1, s & 1


def route(where):
    every = itertools.product(range(4), range(4), range(8), range(2))
    return [(flat(*at), flat(*where(*at))) for at in every]


def swap(block):
    return lax.ppermute(block, BOTH, route(lambda x, y, z, c: (x, y, z, 1 - c)))


def crossed(block, d, swapped):
    def where(x, y, z, c):
        if c == swapped:
            return ((x + d) % 4, y, z, c)
        return (x, (y + d) % 4, z, c)

    return lax.ppermute(block, BOTH, route(where))


def trade_z(blocks):
    groups = [[z * 2 + low_y for z in range(8)] for low_y in range(2)]
    return lax.all_to_all(blocks, "batch", 0, 0, tiled=True, axis_index_groups=groups)


def trade_space(blocks):
    groups = [[chip * 2 + c for chip in range(8)] for c in range(2)]
    return lax.all_to_all(blocks, "space", 0, 0, tiled=True, axis_index_groups=groups)


def at(array, index):
    return lax.dynamic_index_in_dim(array, index, 0, keepdims=False)


def attention_kernel(q_ref, k_ref, v_ref, g_ref, mask_ref, attn_ref, grad_ref):
    full = jnp.float32
    size = 64
    scale = 1.0 / math.sqrt(size)
    over_rows = (((0,), (0,)), ((), ()))
    over_columns = (((1,), (1,)), ((), ()))
    mask = mask_ref[0]
    for head in range(2):
        part = slice(head * size, (head + 1) * size)
        q, k, v, g = q_ref[:, part], k_ref[:, part], v_ref[:, part], g_ref[:, part]
        scores = lax.dot_general(k, q, over_columns, preferred_element_type=full) * scale + mask
        exponent = jnp.exp(scores - jnp.max(scores, 0, keepdims=True))
        probability = exponent * (1.0 / jnp.sum(exponent, 0, keepdims=True))
        low = probability.astype(jnp.bfloat16)
        grad = lax.dot_general(v, g, over_columns, preferred_element_type=full)
        centre = jnp.sum(probability * grad, 0, keepdims=True)
        score_low = (probability * (grad - centre)).astype(jnp.bfloat16)
        attn_ref[:, part] = lax.dot_general(
            low, v, over_rows, preferred_element_type=full
        ).astype(jnp.bfloat16)
        grad_ref[0, :, part] = (
            lax.dot_general(score_low, k, over_rows, preferred_element_type=full) * scale
        ).astype(jnp.bfloat16)
        grad_ref[1, :, part] = (jnp.dot(score_low, q, preferred_element_type=full) * scale).astype(
            jnp.bfloat16
        )
        grad_ref[2, :, part] = jnp.dot(low, g, preferred_element_type=full).astype(jnp.bfloat16)


def attend(qkv, dout, mask):
    rows, width = dout.shape
    pairs = width // 128

    def columns(offset):
        return pl.BlockSpec((ROWS, 128), lambda w, j: (w, offset + j))

    work = 2 * pairs * 2
    return pl.pallas_call(
        attention_kernel,
        grid=(2, pairs),
        in_specs=[
            columns(0),
            columns(pairs),
            columns(2 * pairs),
            columns(0),
            pl.BlockSpec((1, ROWS, ROWS), lambda w, j: (w, 0, 0)),
        ],
        out_specs=[columns(0), pl.BlockSpec((3, ROWS, 128), lambda w, j: (0, w, j))],
        out_shape=[
            jax.ShapeDtypeStruct((rows, width), jnp.bfloat16),
            jax.ShapeDtypeStruct((3, rows, width), jnp.bfloat16),
        ],
        cost_estimate=pl.CostEstimate(
            flops=work * 14 * ROWS * ROWS * 64 * 4,
            bytes_accessed=8 * rows * width * 2,
            transcendentals=work * ROWS * ROWS,
        ),
        compiler_params=pltpu.CompilerParams(vmem_limit_bytes=32 * 2**20),
    )(qkv, qkv, qkv, dout, mask)


LIMIT = pltpu.CompilerParams(vmem_limit_bytes=40 * 2**20)


def cost(flops, bytes_accessed):
    return pl.CostEstimate(flops=flops, bytes_accessed=bytes_accessed, transcendentals=0)


def follow(array, after):
    return pl.pallas_call(
        lambda *refs: None,
        in_specs=[pl.BlockSpec(memory_space=pl.ANY)] * (1 + len(after)),
        out_specs=pl.BlockSpec(memory_space=pl.ANY),
        out_shape=jax.ShapeDtypeStruct(array.shape, array.dtype),
        input_output_aliases={0: 0},
        cost_estimate=cost(0, 0),
    )(array, *after)


def project_kernel(hidden_ref, weight_ref, bias_ref, out_ref):
    out_ref[...] = (
        jnp.dot(hidden_ref[...], weight_ref[0], preferred_element_type=jnp.float32) + bias_ref[...]
    ).astype(jnp.bfloat16)


def project(hidden, weights, biases):
    rows, width = hidden.shape
    return pl.pallas_call(
        project_kernel,
        grid=(6,),
        in_specs=[
            pl.BlockSpec((rows, width), lambda i: (0, 0)),
            pl.BlockSpec((1, width, 256), lambda i: (i, 0, 0)),
            pl.BlockSpec((1, 256), lambda i: (0, i)),
        ],
        out_specs=pl.BlockSpec((rows, 256), lambda i: (0, i)),
        out_shape=jax.ShapeDtypeStruct((rows, 1536), jnp.bfloat16),
        cost_estimate=cost(2 * rows * width * 1536, 8 * 2**20),
        compiler_params=LIMIT,
    )(hidden, weights, biases)


def dout_kernel(grad_ref, kept_ref, got_ref, out_ref):
    total = 0.0
    for i, block in enumerate((kept_ref[0], kept_ref[1], got_ref[0], got_ref[1])):
        total = total + lax.dot_general(
            grad_ref[:, i * 256 : (i + 1) * 256],
            block,
            (((1,), (1,)), ((), ())),
            preferred_element_type=jnp.float32,
        )
    out_ref[...] = total.astype(jnp.bfloat16)


def find_dout(grads, kept, got):
    rows = grads.shape[0]
    return pl.pallas_call(
        dout_kernel,
        out_shape=jax.ShapeDtypeStruct((rows, 512), jnp.bfloat16),
        cost_estimate=cost(2 * rows * 1024 * 512, 4 * 2**20),
        compiler_params=LIMIT,
    )(grads, kept, got)


def terms_kernel(left_ref, right_ref, out_ref):
    out_ref[0] = jnp.dot(left_ref[...], right_ref[0], preferred_element_type=jnp.float32).astype(
        jnp.bfloat16
    )


def find_terms(hidden_t, grad_qkv):
    width, rows = hidden_t.shape
    return pl.pallas_call(
        terms_kernel,
        grid=(6,),
        in_specs=[
            pl.BlockSpec((width, rows), lambda i: (0, 0)),
            pl.BlockSpec((1, rows, 256), lambda i: (i // 2, 0, i % 2)),
        ],
        out_specs=pl.BlockSpec((1, width, 256), lambda i: (i, 0, 0)),
        out_shape=jax.ShapeDtypeStruct((8, width, 256), jnp.bfloat16),
        cost_estimate=cost(2 * rows * width * 1536, 8 * 2**20),
        compiler_params=LIMIT,
    )(hidden_t, grad_qkv)


def last_terms_kernel(left_ref, right_ref, terms_ref, out_ref):
    out_ref[0] = lax.dot_general(
        left_ref[...], right_ref[...], (((0,), (0,)), ((), ())), preferred_element_type=jnp.float32
    ).astype(jnp.bfloat16)


def add_last_terms(attn, grads, terms):
    rows, width = attn.shape
    return pl.pallas_call(
        last_terms_kernel,
        grid=(2,),
        in_specs=[
            pl.BlockSpec((rows, width), lambda i: (0, 0)),
            pl.BlockSpec((rows, 256), lambda i: (0, i)),
            pl.BlockSpec(memory_space=pl.ANY),
        ],
        out_specs=pl.BlockSpec((1, width, 256), lambda i: (6 + i, 0, 0)),
        out_shape=jax.ShapeDtypeStruct(terms.shape, terms.dtype),
        input_output_aliases={2: 0},
        cost_estimate=cost(2 * rows * width * 512, 4 * 2**20),
        compiler_params=LIMIT,
    )(attn, grads, terms)


def hidden_grad_kernel(grad_ref, weight_ref, normed_ref, *rest):
    out_ref, gain_ref, bias_ref = rest[-3:]
    step = pl.program_id(0)
    grad = grad_ref[0]
    bias_ref[0] = jnp.sum(grad.astype(jnp.float32), 0, keepdims=True)
    part = lax.dot_general(
        grad, weight_ref[0], (((1,), (1,)), ((), ())), preferred_element_type=jnp.float32
    )

    @pl.when(step == 0)
    def _():
        out_ref[...] = part

    @pl.when(step > 0)
    def _():
        out_ref[...] += part

    @pl.when(step == 5)
    def _():
        gain_ref[...] = jnp.sum(out_ref[...] * normed_ref[...], 0, keepdims=True)


def find_hidden_grad(grad_qkv, weights, normed, after):
    rows, width = normed.shape
    return pl.pallas_call(
        hidden_grad_kernel,
        grid=(6,),
        in_specs=[
            pl.BlockSpec((1, rows, 256), lambda i: (i // 2, 0, i % 2)),
            pl.BlockSpec((1, width, 256), lambda i: (i, 0, 0)),
            pl.BlockSpec((rows, width), lambda i: (0, 0)),
        ]
        + [pl.BlockSpec(memory_space=pl.ANY)] * len(after),
        out_specs=[
            pl.BlockSpec((rows, width), lambda i: (0, 0)),
            pl.BlockSpec((1, width), lambda i: (0, 0)),
            pl.BlockSpec((1, 1, 256), lambda i: (i, 0, 0)),
        ],
        out_shape=[
            jax.ShapeDtypeStruct((rows, width), jnp.float32),
            jax.ShapeDtypeStruct((1, width), jnp.float32),
            jax.ShapeDtypeStruct((6, 1, 256), jnp.float32),
        ],
        cost_estimate=cost(2 * rows * width * 1536, 14 * 2**20),
        compiler_params=LIMIT,
    )(grad_qkv, weights, normed, *after)


def per_device(inputs, grad_out, fluid, w_qkv, qkv_bias, w_proj, ln_gain):
    full, low = jnp.float32, jnp.bfloat16
    width = w_proj.shape[1]
    half = width // 2
    x, y, z, core = places()
    first = core == 0
    own_rows = w_qkv.shape[0]
    n_space = lax.axis_size("space")
    zero = jnp.uint32(0)

    def block_of(x, y):
        return jnp.where(first, x * 2 + (y >> 1), (y >> 1) * 4 + x)

    def quarter_of(inner):
        return jnp.where(first, (inner & 1) * 2 + (inner >> 1), inner)

    def pairs_of(outer):
        columns = jnp.where(first, outer, outer & 2)
        low_y = jnp.where(first, zero, outer & 1)
        return (columns, low_y), (columns + core, low_y + (1 - core))

    inner_at, outer_at = jnp.where(first, y, x), jnp.where(first, x, y)

    def back(block):
        return lax.ppermute(block, "space", [((i + 1) % n_space, i) for i in range(n_space)])

    walls_plane = jnp.pad(
        fluid[:SHIFT].transpose(1, 2, 0).astype(low), ((0, 0), (0, 0), (0, width - SHIFT))
    )
    rims = back(
        jnp.concatenate([inputs[:, :SHIFT], grad_out[:, :SHIFT], walls_plane[None, None]], 1)
    )
    rim_x, rim_g = rims[:, :SHIFT], rims[:, SHIFT : 2 * SHIFT]
    rim_f = rims[0, 2 * SHIFT, :, :, :SHIFT].transpose(2, 0, 1).astype(fluid.dtype)
    tile_x = jnp.roll(jnp.concatenate([inputs[:, SHIFT:], rim_x], 1), (-SHIFT, -SHIFT), (2, 3))
    tile_g = jnp.roll(jnp.concatenate([grad_out[:, SHIFT:], rim_g], 1), (-SHIFT, -SHIFT), (2, 3))
    tile_f = jnp.roll(jnp.concatenate([fluid[SHIFT:], rim_f], 0), (-SHIFT, -SHIFT), (1, 2))
    extra = ((0, ROWS - TOKENS), (0, 0))
    rows_x = jnp.pad(tile_x.reshape(-1, width), extra)
    rows_g = jnp.pad(tile_g.reshape(-1, width), extra)
    both_x = jnp.concatenate([rows_x, swap(rows_x)], 0).astype(full)
    walls_row = jnp.pad(tile_f.reshape(1, -1).astype(low), ((0, 0), (0, width - TOKENS)))
    padding = jnp.zeros((ROWS - TOKENS - 1, width), low)
    got_g = swap(jnp.concatenate([tile_g.reshape(-1, width), walls_row, padding], 0))
    other_f = got_g[TOKENS, :TOKENS].astype(fluid.dtype)
    grads = jnp.concatenate([rows_g, jnp.pad(got_g[:TOKENS], extra)], 0)
    average = jnp.mean(both_x, -1, keepdims=True)
    centred = both_x - average
    variance = jnp.mean(centred * centred, -1, keepdims=True)
    inv_std = 1.0 / jnp.sqrt(variance + EPS)
    normed = centred * inv_std
    hidden = (normed * ln_gain).astype(low)
    hidden_t = hidden.T
    grads_own_first = jnp.where(
        first, grads, jnp.concatenate([grads[:, half:], grads[:, :half]], 1)
    )

    steps = jnp.arange(WIN, dtype=jnp.int32)
    inner = jnp.where(steps < WIN - SHIFT, 1, 2).astype(jnp.int32)
    last_pair = (x == 3) & (y >= 2)

    def masked(walls, is_last):
        along = jnp.where(is_last, inner, 0)
        labels = along[:, None, None] * 9 + inner[None, :, None] * 3 + inner[None, None, :]
        labels = jnp.pad(labels.reshape(-1), (0, ROWS - TOKENS), constant_values=-1)
        open_keys = jnp.pad(walls.reshape(-1) == 1, (0, ROWS - TOKENS))
        allowed = (labels[:, None] == labels[None, :]) & (
            open_keys[:, None] | jnp.eye(ROWS, dtype=bool)
        )
        return jnp.where(allowed, 0.0, NEG).astype(full)

    mask = jnp.stack([masked(tile_f, last_pair & ~first), masked(other_f, last_pair & first)])

    qkv_parts = w_qkv.reshape(own_rows, 3, 2, half)
    mine = jnp.concatenate(
        [jnp.where(first, qkv_parts[:, i, 0], qkv_parts[:, i, 1]) for i in range(3)]
        + [jnp.where(first, w_proj[:, :half], w_proj[:, half:])],
        1,
    )
    share = lax.dynamic_slice(mine, (zero, block_of(x, y) * 256), (own_rows, 256))
    lined = trade_z(jnp.broadcast_to(share, (8, own_rows, 256)))
    quarters = jnp.zeros((4, 8, own_rows, 256), low)
    for d in range(4):
        piece = crossed(lined, d, 1) if d else lined
        quarters = lax.dynamic_update_slice(
            quarters, piece[None], (quarter_of((inner_at - d) & 3), zero, zero, zero)
        )
    weights = jnp.zeros((4, 2, 8, 2, own_rows, 256), low)
    for d in range(4):
        piece = crossed(quarters, d, 0) if d else quarters
        if d == 1:
            piece = follow(piece, (hidden_t, mask, grads_own_first))
        for i, (columns, low_y) in enumerate(pairs_of((outer_at - d) & 3)):
            weights = lax.dynamic_update_slice(
                weights,
                piece[2 * i : 2 * i + 2].reshape(1, 2, 8, 1, own_rows, 256),
                (columns, zero, zero, low_y, zero, zero),
            )
    weights = weights.reshape(8, width, 256)
    proj = weights[6:]
    kept = lax.dynamic_slice(proj, (zero, core * half, zero), (2, half, 256))
    got = swap(lax.dynamic_slice(proj, (zero, (1 - core) * half, zero), (2, half, 256)))

    biases = qkv_bias.reshape(3, 2, half)
    biases = jnp.where(first, biases[:, 0], biases[:, 1]).reshape(1, -1)
    qkv = project(hidden, weights, biases)
    dout = find_dout(grads_own_first, kept, got)
    attn, grad_qkv = attend(qkv, dout, mask)

    attn_got = swap(attn)
    attn_got = jnp.concatenate([attn_got[ROWS:], attn_got[:ROWS]], 0)
    attn_all = jnp.where(
        first, jnp.concatenate([attn, attn_got], 1), jnp.concatenate([attn_got, attn], 1)
    )
    terms = add_last_terms(attn_all, grads_own_first, find_terms(hidden_t, grad_qkv))
    terms = terms.reshape(4, 2, 8, 2, own_rows, 256)

    def outer_piece(coordinate):
        return jnp.concatenate(
            [
                lax.dynamic_slice(
                    terms, (columns, zero, zero, low_y, zero, zero), (1, 2, 8, 1, own_rows, 256)
                ).reshape(2, 8, own_rows, 256)
                for columns, low_y in pairs_of(coordinate)
            ],
            0,
        )

    pieces = [outer_piece((outer_at + d) & 3) for d in range(4)]
    sums = pieces[0].astype(full)
    for d in range(1, 4):
        sums = sums + crossed(pieces[d], d, 0).astype(full)
    sums = sums.astype(low)

    partial, gain_term, bias_term = find_hidden_grad(grad_qkv, weights, normed, pieces[1:])
    bias_term = bias_term.reshape(3, 1, half)
    nothing = jnp.zeros_like(bias_term)
    bias_term = jnp.where(
        first,
        jnp.concatenate([bias_term, nothing], 1),
        jnp.concatenate([nothing, bias_term], 1),
    )
    small = jnp.concatenate([gain_term.reshape(-1), bias_term.reshape(-1)]).reshape(16, 256)
    small = small + swap(small)

    def split(values):
        upper = lax.reduce_precision(values, 8, 7)
        return jnp.concatenate([upper.astype(low), (values - upper).astype(low)], 0)

    def joined(rows):
        return rows[-32:-16].astype(full) + rows[-16:].astype(full)

    def with_small(rows, extra_rows):
        return jnp.concatenate([rows.reshape(-1, 256), extra_rows], 0)

    extra_rows = split(small)
    total = at(sums, quarter_of(inner_at)).reshape(-1, 256).astype(full)
    for d in range(1, 4):
        piece = at(sums, quarter_of((inner_at + d) & 3))
        arrived = crossed(with_small(piece, extra_rows), d, 1)
        total = total + arrived[:-32].astype(full)
        small = small + joined(arrived)
    sums = total.astype(low).reshape(8, own_rows, 256)
    repeated = jnp.broadcast_to(split(small), (8, 32, 256))
    arrived = trade_z(jnp.concatenate([sums, repeated], 1))
    small = jnp.sum(arrived[:, own_rows:].astype(full), 0)
    small = small[:16] + small[16:]
    final = with_small(
        jnp.sum(arrived[:, :own_rows].astype(full), 0).astype(low), split(small)
    )
    arrived = trade_space(jnp.broadcast_to(final, (8, own_rows + 32, 256)))
    small = jnp.sum(arrived[:4, own_rows:].astype(full), 0)
    small = small[:16] + small[16:]
    rows = arrived[:, :own_rows]
    rows = jnp.where(
        first, rows.reshape(2, 4, own_rows, 256).swapaxes(0, 1).reshape(rows.shape), rows
    )
    others = swap(rows)
    small_got = swap(small)
    small = jnp.where(first, small, small_got).reshape(-1)
    sides = (jnp.where(first, rows, others), jnp.where(first, others, rows))
    blocks = [side[2 * i + j].astype(full) for i in range(4) for side in sides for j in range(2)]
    out_qkv = jnp.concatenate(blocks[:12], 1)
    out_proj = jnp.concatenate(blocks[12:], 1)

    grad_hidden = partial[:ROWS] + swap(partial[ROWS:])
    grad_norm = grad_hidden * ln_gain
    own_normed = normed[:ROWS]
    grad_flat = rows_g.astype(full) + inv_std[:ROWS] * (
        grad_norm
        - jnp.mean(grad_norm, -1, keepdims=True)
        - own_normed * jnp.mean(grad_norm * own_normed, -1, keepdims=True)
    )
    grad_tile = jnp.roll(
        grad_flat[:TOKENS].astype(low).reshape(tile_x.shape), (SHIFT, SHIFT), (2, 3)
    )
    returned = lax.ppermute(
        grad_tile[:, WIN - SHIFT :], "space", [(i, (i + 1) % n_space) for i in range(n_space)]
    )
    grad_input = jnp.concatenate([returned, grad_tile[:, : WIN - SHIFT]], 1)
    return (grad_input, out_qkv, out_proj, small[:width], small[width:])


def solution(mesh):
    tokens = P("batch", "space", None, None, None)
    return jax.shard_map(
        per_device,
        mesh=mesh,
        in_specs=(tokens, tokens, P("space", None, None), P("batch", None), P(), P("batch", None), P()),
        out_specs=(tokens, P("batch", None), P("batch", None), P(), P()),
        check_vma=False,
    )
```

profile of v0, /device:TPU:1, one launch (start us, length us, event | category | flops | bytes accessed | tf_op | source)
XLA Modules:
  0.0 206.8 jit_solution(15262692877092702968)
XLA Ops:
  2.8 3.2 %collective-permute-start = (bf16[1,7,7,7,1024]{4,3,2,1,0:T(8,128)(2,1)}, bf16[1,7,7,7,1024]{4,3,2,1,0:T(8,128)(2,1)}, u32[]{:S(2)}, u32[]{:S(2)}) collective-permute-start(bf16[1,7,7,7,1024]{4,3,2,1,0:T(8,128)(2,1)} %pad_maximum_fusion.10), channel_id=1, source_target_pairs={{16,0},{32,16},{48,32},{64,48},{80,64},{96,80},{112,96},{128,112},... | collective-permute-start | bytes 2107400 | tf_op jit(solution)/shard_map/ppermute | solution.py:305
  7.9 6.4 %all-to-all-start = ((bf16[8,64,256]{2,1,0:T(8,128)(2,1)}), bf16[8,64,256]{2,1,0:T(8,128)(2,1)S(1)}, u32[]{:S(2)}, u32[]{:S(2)}) async-start(bf16[8,64,256]{2,1,0:T(8,128)(2,1)} %broadcast_in_dim.78), calls=%async_computation | async-start | bytes 524288 | tf_op jit(solution)/shard_map/all_to_all | solution.py:51
  15.2 8.5 %all-to-all-done = bf16[8,64,256]{2,1,0:T(8,128)(2,1)S(1)} async-done(((bf16[8,64,256]{2,1,0:T(8,128)(2,1)}), bf16[8,64,256]{2,1,0:T(8,128)(2,1)S(1)}, u32[]{:S(2)}, u32[]{:S(2)}) %all-to-all-start) | async-done | bytes 262176 | tf_op jit(solution)/shard_map/all_to_all | solution.py:51
  23.7 4.2 %collective-permute-start.2 = (bf16[8,64,256]{2,1,0:T(8,128)(2,1)S(1)}, bf16[8,64,256]{2,1,0:T(8,128)(2,1)}, u32[]{:S(2)}, u32[]{:S(2)}) collective-permute-start(bf16[8,64,256]{2,1,0:T(8,128)(2,1)S(1)} %all-to-all-done), channel_id=1, source_target_pairs={{0,1},{16,48},{2,3},{18,50},{4,5},{20,52},{6,7},{22,54},{8,9},{24,... | collective-permute-start | bytes 786440 | tf_op jit(solution)/shard_map/ppermute | solution.py:46
  51.6 2.0 collective-permute-start.8
  61.6 2.1 %multiply_convert_fusion = (bf16[704,1024]{1,0:T(8,128)(2,1)S(1)}, f32[704,1024]{1,0:T(8,128)}) fusion(f32[1024]{0:T(1024)S(1)} %copy-done.19, f32[704]{0:T(1024)S(1)} %add_rsqrt_fusion, f32[704]{0:T(1024)S(1)} %broadcast_multiply_fusion, bf16[352,1024]{1,0:T(8,128)(2,1)S(1)} %collective-permute-done.1, bf16[352,1024]{1,0:T(8,128)(2,1)S(1)} %pad.36), kind=kLoop, calls=%fused_computation.5 | loop fusion | flops 5767168 | bytes 5776896 | tf_op jit(solution)/shard_map/convert_element_type | solution.py:332
  66.3 1.9 fusion.28
  68.2 1.9 fusion.27
  70.1 5.6 %collective-permute-done.7 = bf16[4,8,64,256]{3,2,1,0:T(8,128)(2,1)} collective-permute-done((bf16[4,8,64,256]{3,2,1,0:T(8,128)(2,1)}, bf16[4,8,64,256]{3,2,1,0:T(8,128)(2,1)}, u32[]{:S(2)}, u32[]{:S(2)}) %collective-permute-start.7) | collective-permute-done | bytes 1048608 | tf_op jit(solution)/shard_map/ppermute | solution.py:46
  75.7 1.9 fusion.26
  77.6 1.9 fusion.25
  81.3 1.9 fusion.23
  85.4 2.1 %collective-permute-start.9 = (bf16[2,512,256]{2,1,0:T(8,128)(2,1)}, bf16[2,512,256]{2,1,0:T(8,128)(2,1)}, u32[]{:S(2)}, u32[]{:S(2)}) collective-permute-start(bf16[2,512,256]{2,1,0:T(8,128)(2,1)} %get-tuple-element.39), channel_id=1, source_target_pairs={{0,16},{16,0},{2,18},{18,2},{4,20},{20,4},{6,22},{22,6},{8,24},{24... | collective-permute-start | bytes 1572872 | tf_op jit(solution)/shard_map/ppermute | solution.py:37
  87.5 2.2 %copy-done.2 = bf16[4,2,8,2,64,256]{5,4,3,2,1,0:T(8,128)(2,1)S(1)} copy-done((bf16[4,2,8,2,64,256]{5,4,3,2,1,0:T(8,128)(2,1)S(1)}, bf16[4,2,8,2,64,256]{5,4,3,2,1,0:T(8,128)(2,1)}, u32[]{:S(2)}) %copy-start.2) | copy-done | bytes 4194328
  89.7 3.4 %shard_map.111.q_ref.k_ref.v_ref = bf16[704,1536]{1,0:T(8,128)(2,1)S(1)} custom-call(bf16[704,1024]{1,0:T(8,128)(2,1)S(1)} %get-tuple-element.31.hidden_ref, bf16[8,1024,256]{2,1,0:T(8,128)(2,1)S(1)} %bitcast.190, f32[1,1536]{1,0:T(1,128)S(1)} %bitcast.193), custom_call_target="tpu_custom_call" | custom-call | flops 2214592512 | bytes 8388608 | tf_op jit(solution)/shard_map/pallas_call | solution.py:150
  93.2 2.1 %shard_map.112.g_ref = bf16[704,512]{1,0:T(8,128)(2,1)S(1)} custom-call(bf16[704,1024]{1,0:T(8,128)(2,1)S(1)} %copy-done, bf16[2,512,256]{2,1,0:T(8,128)(2,1)S(1)} %get-tuple-element.40.kept_ref, bf16[2,512,256]{2,1,0:T(8,128)(2,1)} %collective-permute-done.9.got_ref), custom_call_target="tpu_custom_call" | custom-call | flops 738197504 | bytes 4194304 | tf_op jit(solution)/shard_map/pallas_call | solution.py:179
  95.3 14.6 %shard_map.113 = (bf16[704,512]{1,0:T(8,128)(2,1)}, bf16[3,704,512]{2,1,0:T(8,128)(2,1)S(1)}) custom-call(bf16[704,1536]{1,0:T(8,128)(2,1)S(1)} %shard_map.111.q_ref.k_ref.v_ref, bf16[704,1536]{1,0:T(8,128)(2,1)S(1)} %shard_map.111.q_ref.k_ref.v_ref, bf16[704,1536]{1,0:T(8,128)(2,1)S(1)} %shard_map.111.q_ref.k_ref.v_ref, ...), custom_call_target="tpu_custom_call" | custom-call | flops 7105150976 | bytes 5767168 | tf_op jit(solution)/shard_map/pallas_call | solution.py:100
  112.8 3.8 %shard_map.114.terms_ref = bf16[8,1024,256]{2,1,0:T(8,128)(2,1)S(1)} custom-call(bf16[1024,704]{1,0:T(8,128)(2,1)S(1)} %copy-done.4, bf16[3,704,512]{2,1,0:T(8,128)(2,1)S(1)} %copy-done.8), custom_call_target="tpu_custom_call" | custom-call | flops 2214592512 | bytes 8388608 | tf_op jit(solution)/shard_map/pallas_call | solution.py:195
  123.5 4.2 %collective-permute-start.15 = (bf16[4,8,64,256]{3,2,1,0:T(8,128)(2,1)}, bf16[4,8,64,256]{3,2,1,0:T(8,128)(2,1)}, u32[]{:S(2)}, u32[]{:S(2)}) collective-permute-start(bf16[4,8,64,256]{3,2,1,0:T(8,128)(2,1)} %pad_maximum_fusion.5.rest_2_), channel_id=1, source_target_pairs={{0,96},{16,145},{2,98},{18,147},{4,100},{20,149},{6,102},{22,151},... | collective-permute-start | bytes 3145736 | tf_op jit(solution)/shard_map/ppermute | solution.py:46
  132.2 7.1 %shard_map.116 = (f32[704,1024]{1,0:T(8,128)S(1)}, f32[1,1024]{1,0:T(1,128)S(1)}, f32[6,1,256]{2,1,0:T(1,128)S(1)}) custom-call(bf16[3,704,512]{2,1,0:T(8,128)(2,1)S(1)} %copy-done.9, bf16[8,1024,256]{2,1,0:T(8,128)(2,1)} %bitcast.189, f32[704,1024]{1,0:T(8,128)S(1)} %copy-done.3, bf16[4,8,64,256]{3,2,1,0:T(8,128)(2,1)} %pad_maximum_fusion.3.rest_0_, ...), custom_call_target="tpu_custom_call" | custom-call | flops 2214592512 | bytes 14680064 | tf_op jit(solution)/shard_map/pallas_call | solution.py:257
  141.1 2.7 %slice.347 = f32[352,1024]{1,0:T(8,128)} slice(f32[704,1024]{1,0:T(8,128)} %copy-done.6), slice={[352:704], [0:1024]} | slice | bytes 2883584 | tf_op jit(solution)/shard_map/slice | solution.py:466
  144.2 6.8 %collective-permute-done.15 = bf16[4,8,64,256]{3,2,1,0:T(8,128)(2,1)} collective-permute-done((bf16[4,8,64,256]{3,2,1,0:T(8,128)(2,1)}, bf16[4,8,64,256]{3,2,1,0:T(8,128)(2,1)}, u32[]{:S(2)}, u32[]{:S(2)}) %collective-permute-start.15) | collective-permute-done | bytes 1048608 | tf_op jit(solution)/shard_map/ppermute | solution.py:46
  151.0 4.8 %collective-permute-done.13 = bf16[4,8,64,256]{3,2,1,0:T(8,128)(2,1)} collective-permute-done((bf16[4,8,64,256]{3,2,1,0:T(8,128)(2,1)}, bf16[4,8,64,256]{3,2,1,0:T(8,128)(2,1)}, u32[]{:S(2)}, u32[]{:S(2)}) %collective-permute-start.13) | collective-permute-done | bytes 1048608 | tf_op jit(solution)/shard_map/ppermute | solution.py:46
  155.8 2.5 %add_convert_fusion = bf16[4,8,64,256]{3,2,1,0:T(8,128)(2,1)S(1)} fusion(bf16[4,8,64,256]{3,2,1,0:T(8,128)(2,1)} %collective-permute-done.15, bf16[4,8,64,256]{3,2,1,0:T(8,128)(2,1)} %collective-permute-done.14, bf16[4,8,64,256]{3,2,1,0:T(8,128)(2,1)} %collective-permute-done.13, bf16[2,8,64,256]{3,2,1,0:T(8,128)(2,1)S(1)} %copy-done.12, ...), kind=kLoop, calls=%fused_computation.8 | loop fusion | flops 4718592 | bytes 5242880 | tf_op jit(solution)/shard_map/convert_element_type | solution.py:413
  160.1 4.2 %collective-permute-done.19 = bf16[544,256]{1,0:T(8,128)(2,1)S(1)} collective-permute-done((bf16[544,256]{1,0:T(8,128)(2,1)S(1)}, bf16[544,256]{1,0:T(8,128)(2,1)S(1)}, u32[]{:S(2)}, u32[]{:S(2)}) %collective-permute-start.19) | collective-permute-done | bytes 278560 | tf_op jit(solution)/shard_map/ppermute | solution.py:46
  166.0 2.9 %collective-permute-done.17 = bf16[544,256]{1,0:T(8,128)(2,1)S(1)} collective-permute-done((bf16[544,256]{1,0:T(8,128)(2,1)S(1)}, bf16[544,256]{1,0:T(8,128)(2,1)S(1)}, u32[]{:S(2)}, u32[]{:S(2)}) %collective-permute-start.17) | collective-permute-done | bytes 278560 | tf_op jit(solution)/shard_map/ppermute | solution.py:46
  169.9 3.5 %all-to-all-start.1 = ((bf16[8,96,256]{2,1,0:T(8,128)(2,1)}), bf16[8,96,256]{2,1,0:T(8,128)(2,1)S(1)}, u32[]{:S(2)}, u32[]{:S(2)}) async-start(bf16[8,96,256]{2,1,0:T(8,128)(2,1)} %pad_maximum_fusion.19), calls=%async_computation.1 | async-start | bytes 786432 | tf_op jit(solution)/shard_map/all_to_all | solution.py:51
  173.4 2.4 %fusion.59 = (f32[352]{0:T(512)S(1)}, f32[352]{0:T(512)S(1)}, f32[352,1024]{1,0:T(8,128)S(1)}, f32[352,1024]{1,0:T(8,128)S(1)}) fusion(f32[704,1024]{1,0:T(8,128)S(1)} %copy-done.3, f32[1024]{0:T(1024)S(1)} %copy-done.19, f32[352,1024]{1,0:T(8,128)} %collective-permute-done.11, f32[704,1024]{1,0:T(8,128)} %copy-done.6), kind=kLoop, calls=%fused_computation.206 | loop fusion | flops 1801536 | bytes 7215872 | tf_op jit(solution)/shard_map/reduce_sum | solution.py:471
  177.9 7.3 %all-to-all-done.1 = bf16[8,96,256]{2,1,0:T(8,128)(2,1)S(1)} async-done(((bf16[8,96,256]{2,1,0:T(8,128)(2,1)}), bf16[8,96,256]{2,1,0:T(8,128)(2,1)S(1)}, u32[]{:S(2)}, u32[]{:S(2)}) %all-to-all-start.1) | async-done | bytes 393248 | tf_op jit(solution)/shard_map/all_to_all | solution.py:51
  186.1 3.5 %all-to-all-start.2 = ((bf16[8,96,256]{2,1,0:T(8,128)(2,1)}), bf16[8,96,256]{2,1,0:T(8,128)(2,1)S(1)}, u32[]{:S(2)}, u32[]{:S(2)}) async-start(bf16[8,96,256]{2,1,0:T(8,128)(2,1)} %broadcast_in_dim.90), calls=%async_computation.2 | async-start | bytes 786432 | tf_op jit(solution)/shard_map/all_to_all | solution.py:56
  190.8 7.1 %all-to-all-done.2 = bf16[8,96,256]{2,1,0:T(8,128)(2,1)S(1)} async-done(((bf16[8,96,256]{2,1,0:T(8,128)(2,1)}), bf16[8,96,256]{2,1,0:T(8,128)(2,1)S(1)}, u32[]{:S(2)}, u32[]{:S(2)}) %all-to-all-start.2) | async-done | bytes 393248 | tf_op jit(solution)/shard_map/all_to_all | solution.py:56
  198.0 4.9 %collective-permute-start.21 = (f32[16,256]{1,0:T(8,128)S(1)}, f32[16,256]{1,0:T(8,128)S(1)}, u32[]{:S(2)}, u32[]{:S(2)}) collective-permute-start(f32[16,256]{1,0:T(8,128)S(1)} %slice_add_fusion.1), channel_id=1, source_target_pairs={{0,16},{16,0},{2,18},{18,2},{4,20},{20,4},{6,22},{22,6},{8,24},{24... | collective-permute-start | bytes 49160 | tf_op jit(solution)/shard_map/ppermute | solution.py:37
  (225 shorter events, 71.3 us)
Async XLA Ops:
  2.8 30.7 %collective-permute-start = (bf16[1,7,7,7,1024]{4,3,2,1,0:T(8,128)(2,1)}, bf16[1,7,7,7,1024]{4,3,2,1,0:T(8,128)(2,1)}, u32[]{:S(2)}, u32[]{:S(2)}) collective-permute-start(bf16[1,7,7,7,1024]{4,3,2,1,0:T(8,128)(2,1)} %pad_maximum_fusion.10), channel_id=1, source_target_pairs={{16,0},{32,16},{48,32},{64,48},{80,64},{96,80},{112,96},{128,112},... | collective-permute-start | bytes 2107400 | tf_op jit(solution)/shard_map/ppermute | solution.py:305
  6.3 8.1 %copy-start.14 = (bf16[1,7,7,7,1024]{4,3,2,1,0:T(8,128)(2,1)S(1)}, bf16[1,7,7,7,1024]{4,3,2,1,0:T(8,128)(2,1)}, u32[]{:S(2)}) copy-start(bf16[1,7,7,7,1024]{4,3,2,1,0:T(8,128)(2,1)} %param.7) | copy-start | bytes 2107396
  7.0 7.4 %copy-start.13 = (bf16[1,7,7,7,1024]{4,3,2,1,0:T(8,128)(2,1)S(1)}, bf16[1,7,7,7,1024]{4,3,2,1,0:T(8,128)(2,1)}, u32[]{:S(2)}) copy-start(bf16[1,7,7,7,1024]{4,3,2,1,0:T(8,128)(2,1)} %param.8) | copy-start | bytes 2107396
  7.1 7.4 %copy-start.17 = (s32[7,7,7]{2,1,0:T(8,128)S(1)}, s32[7,7,7]{2,1,0:T(8,128)}, u32[]{:S(2)}) copy-start(s32[7,7,7]{2,1,0:T(8,128)} %param.9) | copy-start | bytes 4120
  7.9 15.8 %all-to-all-start = ((bf16[8,64,256]{2,1,0:T(8,128)(2,1)}), bf16[8,64,256]{2,1,0:T(8,128)(2,1)S(1)}, u32[]{:S(2)}, u32[]{:S(2)}) async-start(bf16[8,64,256]{2,1,0:T(8,128)(2,1)} %broadcast_in_dim.78), calls=%async_computation | async-start | bytes 524288 | tf_op jit(solution)/shard_map/all_to_all | solution.py:51
  23.7 20.2 %collective-permute-start.2 = (bf16[8,64,256]{2,1,0:T(8,128)(2,1)S(1)}, bf16[8,64,256]{2,1,0:T(8,128)(2,1)}, u32[]{:S(2)}, u32[]{:S(2)}) collective-permute-start(bf16[8,64,256]{2,1,0:T(8,128)(2,1)S(1)} %all-to-all-done), channel_id=1, source_target_pairs={{0,1},{16,48},{2,3},{18,50},{4,5},{20,52},{6,7},{22,54},{8,9},{24,... | collective-permute-start | bytes 786440 | tf_op jit(solution)/shard_map/ppermute | solution.py:46
  27.9 17.6 %collective-permute-start.3 = (bf16[8,64,256]{2,1,0:T(8,128)(2,1)S(1)}, bf16[8,64,256]{2,1,0:T(8,128)(2,1)}, u32[]{:S(2)}, u32[]{:S(2)}) collective-permute-start(bf16[8,64,256]{2,1,0:T(8,128)(2,1)S(1)} %all-to-all-done), channel_id=1, source_target_pairs={{0,128},{16,80},{2,130},{18,82},{4,132},{20,84},{6,134},{22,86},{8... | collective-permute-start | bytes 786440 | tf_op jit(solution)/shard_map/ppermute | solution.py:46
  29.8 17.4 %collective-permute-start.4 = (bf16[8,64,256]{2,1,0:T(8,128)(2,1)S(1)}, bf16[8,64,256]{2,1,0:T(8,128)(2,1)}, u32[]{:S(2)}, u32[]{:S(2)}) collective-permute-start(bf16[8,64,256]{2,1,0:T(8,128)(2,1)S(1)} %all-to-all-done), channel_id=1, source_target_pairs={{0,129},{16,112},{2,131},{18,114},{4,133},{20,116},{6,135},{22,118... | collective-permute-start | bytes 786440 | tf_op jit(solution)/shard_map/ppermute | solution.py:46
  37.7 18.6 %collective-permute-start.1 = (bf16[352,1024]{1,0:T(8,128)(2,1)S(1)}, bf16[352,1024]{1,0:T(8,128)(2,1)S(1)}, u32[]{:S(2)}, u32[]{:S(2)}) collective-permute-start(bf16[352,1024]{1,0:T(8,128)(2,1)S(1)} %pad.36), channel_id=1, source_target_pairs={{0,16},{16,0},{2,18},{18,2},{4,20},{20,4},{6,22},{22,6},{8,24},{24... | collective-permute-start | bytes 2162696 | tf_op jit(solution)/shard_map/ppermute | solution.py:37
  43.5 13.1 %collective-permute-start.6 = (bf16[352,1024]{1,0:T(8,128)(2,1)}, bf16[352,1024]{1,0:T(8,128)(2,1)}, u32[]{:S(2)}, u32[]{:S(2)}) collective-permute-start(bf16[352,1024]{1,0:T(8,128)(2,1)} %get-tuple-element.46), channel_id=1, source_target_pairs={{0,16},{16,0},{2,18},{18,2},{4,20},{20,4},{6,22},{22,6},{8,24},{24... | collective-permute-start | bytes 2162696 | tf_op jit(solution)/shard_map/ppermute | solution.py:37
  49.0 17.3 %collective-permute-start.5 = (bf16[4,8,64,256]{3,2,1,0:T(8,128)(2,1)}, bf16[4,8,64,256]{3,2,1,0:T(8,128)(2,1)}, u32[]{:S(2)}, u32[]{:S(2)}) collective-permute-start(bf16[4,8,64,256]{3,2,1,0:T(8,128)(2,1)} %bitcast_dynamic-update-slice_fusion), channel_id=1, source_target_pairs={{0,32},{16,17},{2,34},{18,19},{4,36},{20,21},{6,38},{22,23},{8,40}... | collective-permute-start | bytes 3145736 | tf_op jit(solution)/shard_map/ppermute | solution.py:46
  49.9 25.7 %collective-permute-start.7 = (bf16[4,8,64,256]{3,2,1,0:T(8,128)(2,1)}, bf16[4,8,64,256]{3,2,1,0:T(8,128)(2,1)}, u32[]{:S(2)}, u32[]{:S(2)}) collective-permute-start(bf16[4,8,64,256]{3,2,1,0:T(8,128)(2,1)} %bitcast_dynamic-update-slice_fusion), channel_id=1, source_target_pairs={{0,64},{16,144},{2,66},{18,146},{4,68},{20,148},{6,70},{22,150},{8... | collective-permute-start | bytes 3145736 | tf_op jit(solution)/shard_map/ppermute | solution.py:46
  51.6 27.8 %collective-permute-start.8 = (bf16[4,8,64,256]{3,2,1,0:T(8,128)(2,1)}, bf16[4,8,64,256]{3,2,1,0:T(8,128)(2,1)}, u32[]{:S(2)}, u32[]{:S(2)}) collective-permute-start(bf16[4,8,64,256]{3,2,1,0:T(8,128)(2,1)} %bitcast_dynamic-update-slice_fusion), channel_id=1, source_target_pairs={{0,96},{16,145},{2,98},{18,147},{4,100},{20,149},{6,102},{22,151},... | collective-permute-start | bytes 3145736 | tf_op jit(solution)/shard_map/ppermute | solution.py:46
  59.7 100.4 %copy-start.18 = (f32[704]{0:T(1024)}, f32[704]{0:T(1024)S(1)}, u32[]{:S(2)}) copy-start(f32[704]{0:T(1024)S(1)} %add_rsqrt_fusion) | copy-start | bytes 8452
  85.4 7.8 %collective-permute-start.9 = (bf16[2,512,256]{2,1,0:T(8,128)(2,1)}, bf16[2,512,256]{2,1,0:T(8,128)(2,1)}, u32[]{:S(2)}, u32[]{:S(2)}) collective-permute-start(bf16[2,512,256]{2,1,0:T(8,128)(2,1)} %get-tuple-element.39), channel_id=1, source_target_pairs={{0,16},{16,0},{2,18},{18,2},{4,20},{20,4},{6,22},{22,6},{8,24},{24... | collective-permute-start | bytes 1572872 | tf_op jit(solution)/shard_map/ppermute | solution.py:37
  95.3 15.9 %copy-start.4 = (bf16[1024,704]{1,0:T(8,128)(2,1)S(1)}, bf16[1024,704]{1,0:T(8,128)(2,1)}, u32[]{:S(2)}) copy-start(bf16[1024,704]{1,0:T(8,128)(2,1)} %copy.145.refs_1_.left_ref) | copy-start | bytes 4325380
  111.2 5.4 %collective-permute-start.10 = (bf16[704,512]{1,0:T(8,128)(2,1)}, bf16[704,512]{1,0:T(8,128)(2,1)}, u32[]{:S(2)}, u32[]{:S(2)}) collective-permute-start(bf16[704,512]{1,0:T(8,128)(2,1)} %get-tuple-element.11), channel_id=1, source_target_pairs={{0,16},{16,0},{2,18},{18,2},{4,20},{20,4},{6,22},{22,6},{8,24},{24... | collective-permute-start | bytes 2162696 | tf_op jit(solution)/shard_map/ppermute | solution.py:37
  122.4 9.7 %copy-start.9 = (bf16[3,704,512]{2,1,0:T(8,128)(2,1)S(1)}, bf16[3,704,512]{2,1,0:T(8,128)(2,1)}, u32[]{:S(2)}) copy-start(bf16[3,704,512]{2,1,0:T(8,128)(2,1)} %copy-done.7) | copy-start | bytes 6488068
  123.5 27.5 %collective-permute-start.15 = (bf16[4,8,64,256]{3,2,1,0:T(8,128)(2,1)}, bf16[4,8,64,256]{3,2,1,0:T(8,128)(2,1)}, u32[]{:S(2)}, u32[]{:S(2)}) collective-permute-start(bf16[4,8,64,256]{3,2,1,0:T(8,128)(2,1)} %pad_maximum_fusion.5.rest_2_), channel_id=1, source_target_pairs={{0,96},{16,145},{2,98},{18,147},{4,100},{20,149},{6,102},{22,151},... | collective-permute-start | bytes 3145736 | tf_op jit(solution)/shard_map/ppermute | solution.py:46
  128.8 22.2 %collective-permute-start.14 = (bf16[4,8,64,256]{3,2,1,0:T(8,128)(2,1)}, bf16[4,8,64,256]{3,2,1,0:T(8,128)(2,1)}, u32[]{:S(2)}, u32[]{:S(2)}) collective-permute-start(bf16[4,8,64,256]{3,2,1,0:T(8,128)(2,1)} %pad_maximum_fusion.4.rest_1_), channel_id=1, source_target_pairs={{0,64},{16,144},{2,66},{18,146},{4,68},{20,148},{6,70},{22,150},{8... | collective-permute-start | bytes 3145736 | tf_op jit(solution)/shard_map/ppermute | solution.py:46
  131.3 24.5 %collective-permute-start.13 = (bf16[4,8,64,256]{3,2,1,0:T(8,128)(2,1)}, bf16[4,8,64,256]{3,2,1,0:T(8,128)(2,1)}, u32[]{:S(2)}, u32[]{:S(2)}) collective-permute-start(bf16[4,8,64,256]{3,2,1,0:T(8,128)(2,1)} %pad_maximum_fusion.3.rest_0_), channel_id=1, source_target_pairs={{0,32},{16,17},{2,34},{18,19},{4,36},{20,21},{6,38},{22,23},{8,40}... | collective-permute-start | bytes 3145736 | tf_op jit(solution)/shard_map/ppermute | solution.py:46
  140.9 3.3 %collective-permute-start.16 = (f32[16,256]{1,0:T(8,128)S(1)}, f32[16,256]{1,0:T(8,128)S(1)}, u32[]{:S(2)}, u32[]{:S(2)}) collective-permute-start(f32[16,256]{1,0:T(8,128)S(1)} %reshape.512), channel_id=1, source_target_pairs={{0,16},{16,0},{2,18},{18,2},{4,20},{20,4},{6,22},{22,6},{8,24},{24... | collective-permute-start | bytes 49160 | tf_op jit(solution)/shard_map/ppermute | solution.py:37
  141.0 14.8 %copy-start.12 = (bf16[2,8,64,256]{3,2,1,0:T(8,128)(2,1)S(1)}, bf16[2,8,64,256]{3,2,1,0:T(8,128)(2,1)}, u32[]{:S(2)}) copy-start(bf16[2,8,64,256]{3,2,1,0:T(8,128)(2,1)} %get-tuple-element.29) | copy-start | bytes 1572868
  143.8 29.6 %collective-permute-start.11 = (f32[352,1024]{1,0:T(8,128)}, f32[352,1024]{1,0:T(8,128)}, u32[]{:S(2)}, u32[]{:S(2)}) collective-permute-start(f32[352,1024]{1,0:T(8,128)} %slice.347), channel_id=1, source_target_pairs={{0,16},{16,0},{2,18},{18,2},{4,20},{20,4},{6,22},{22,6},{8,24},{24... | collective-permute-start | bytes 4325384 | tf_op jit(solution)/shard_map/ppermute | solution.py:37
  158.6 5.8 %collective-permute-start.19 = (bf16[544,256]{1,0:T(8,128)(2,1)S(1)}, bf16[544,256]{1,0:T(8,128)(2,1)S(1)}, u32[]{:S(2)}, u32[]{:S(2)}) collective-permute-start(bf16[544,256]{1,0:T(8,128)(2,1)S(1)} %get-tuple-element.60), channel_id=1, source_target_pairs={{0,129},{16,112},{2,131},{18,114},{4,133},{20,116},{6,135},{22,118... | collective-permute-start | bytes 835592 | tf_op jit(solution)/shard_map/ppermute | solution.py:46
  158.7 7.3 %collective-permute-start.18 = (bf16[544,256]{1,0:T(8,128)(2,1)S(1)}, bf16[544,256]{1,0:T(8,128)(2,1)S(1)}, u32[]{:S(2)}, u32[]{:S(2)}) collective-permute-start(bf16[544,256]{1,0:T(8,128)(2,1)S(1)} %get-tuple-element.59), channel_id=1, source_target_pairs={{0,128},{16,80},{2,130},{18,82},{4,132},{20,84},{6,134},{22,86},{8... | collective-permute-start | bytes 835592 | tf_op jit(solution)/shard_map/ppermute | solution.py:46
  158.8 10.2 %collective-permute-start.17 = (bf16[544,256]{1,0:T(8,128)(2,1)S(1)}, bf16[544,256]{1,0:T(8,128)(2,1)S(1)}, u32[]{:S(2)}, u32[]{:S(2)}) collective-permute-start(bf16[544,256]{1,0:T(8,128)(2,1)S(1)} %get-tuple-element.58), channel_id=1, source_target_pairs={{0,1},{16,48},{2,3},{18,50},{4,5},{20,52},{6,7},{22,54},{8,9},{24,... | collective-permute-start | bytes 835592 | tf_op jit(solution)/shard_map/ppermute | solution.py:46
  169.9 15.3 %all-to-all-start.1 = ((bf16[8,96,256]{2,1,0:T(8,128)(2,1)}), bf16[8,96,256]{2,1,0:T(8,128)(2,1)S(1)}, u32[]{:S(2)}, u32[]{:S(2)}) async-start(bf16[8,96,256]{2,1,0:T(8,128)(2,1)} %pad_maximum_fusion.19), calls=%async_computation.1 | async-start | bytes 786432 | tf_op jit(solution)/shard_map/all_to_all | solution.py:51
  177.1 12.5 %collective-permute-start.12 = (bf16[1,3,7,7,1024]{4,3,2,1,0:T(8,128)(2,1)S(1)}, bf16[1,3,7,7,1024]{4,3,2,1,0:T(8,128)(2,1)S(1)}, u32[]{:S(2)}, u32[]{:S(2)}) collective-permute-start(bf16[1,3,7,7,1024]{4,3,2,1,0:T(8,128)(2,1)S(1)} %pad_maximum_fusion.20), channel_id=1, source_target_pairs={{0,16},{16,32},{32,48},{48,64},{64,80},{80,96},{96,112},{112,128},... | collective-permute-start | bytes 903176 | tf_op jit(solution)/shard_map/ppermute | solution.py:477
  186.1 11.7 %all-to-all-start.2 = ((bf16[8,96,256]{2,1,0:T(8,128)(2,1)}), bf16[8,96,256]{2,1,0:T(8,128)(2,1)S(1)}, u32[]{:S(2)}, u32[]{:S(2)}) async-start(bf16[8,96,256]{2,1,0:T(8,128)(2,1)} %broadcast_in_dim.90), calls=%async_computation.2 | async-start | bytes 786432 | tf_op jit(solution)/shard_map/all_to_all | solution.py:56
  198.0 5.7 %collective-permute-start.21 = (f32[16,256]{1,0:T(8,128)S(1)}, f32[16,256]{1,0:T(8,128)S(1)}, u32[]{:S(2)}, u32[]{:S(2)}) collective-permute-start(f32[16,256]{1,0:T(8,128)S(1)} %slice_add_fusion.1), channel_id=1, source_target_pairs={{0,16},{16,0},{2,18},{18,2},{4,20},{20,4},{6,22},{22,6},{8,24},{24... | collective-permute-start | bytes 49160 | tf_op jit(solution)/shard_map/ppermute | solution.py:37
  202.9 2.0 collective-permute-start.20
  (18 other events, 48.1 us)
where the time goes:
time: 208 us; the launch traced here: 207 us
  waiting for transfers between devices  49.7 us (24%)
  starting transfers between devices  47.5 us (23%)
  local copies, waits for them, and re-layouts  45.7 us (22%)
  Pallas kernels  32.4 us (16%)
  other arithmetic  29.7 us (14%)
    ppermute x12, waiting for transfers between devices, crossed(): return lax.ppermute(block, BOTH, route(where))  26 us
    ppermute x12, starting transfers between devices, crossed(): return lax.ppermute(block, BOTH, route(where))  20.5 us
    all_to_all x2, waiting for transfers between devices, trade_z(): lax.all_to_all(blocks, 'batch', 0, 0, tiled=True, axis_index_groups=groups)  15.9 us
    pallas_call x1, Pallas kernels, attend(): pl.pallas_call(attention_kernel, grid=(2, pairs), in_specs=[columns(0), c...  14.6 us
    dynamic_update_slice x8, local copies, waits for them, and re-layouts, per_device(): lax.dynamic_update_slice(weights, piece[2 * i:2 * i + 2].reshape(1, 2, 8,...  13.5 us
    all_to_all x2, starting transfers between devices, trade_z(): lax.all_to_all(blocks, 'batch', 0, 0, tiled=True, axis_index_groups=groups)  9.9 us
    ppermute x8, starting transfers between devices, swap(): return lax.ppermute(block, BOTH, route(lambda x, y, z, c: (x, y, z, 1 - c)))  9.52 us
    unnamed x61, local copies, waits for them, and re-layouts  7.59 us
  transfers between devices with their start and end apart: 25, of which 10 were waited for; matrix products, arithmetic and copies ran while one was open for 26% of the time, Pallas kernels for 7%

commit v1 on v0

--- a/solution.py
+++ b/solution.py
@@ -67,26 +67,27 @@
     over_rows = (((0,), (0,)), ((), ()))
     over_columns = (((1,), (1,)), ((), ()))
     mask = mask_ref[0]
+    for_queries = []
     for head in range(2):
         part = slice(head * size, (head + 1) * size)
         q, k, v, g = q_ref[:, part], k_ref[:, part], v_ref[:, part], g_ref[:, part]
-        scores = lax.dot_general(k, q, over_columns, preferred_element_type=full) * scale + mask
+        scaled = q * jnp.bfloat16(scale)
+        scores = lax.dot_general(k, scaled, over_columns, preferred_element_type=full) + mask
         exponent = jnp.exp(scores - jnp.max(scores, 0, keepdims=True))
         probability = exponent * (1.0 / jnp.sum(exponent, 0, keepdims=True))
         low = probability.astype(jnp.bfloat16)
         grad = lax.dot_general(v, g, over_columns, preferred_element_type=full)
         centre = jnp.sum(probability * grad, 0, keepdims=True)
         score_low = (probability * (grad - centre)).astype(jnp.bfloat16)
-        attn_ref[:, part] = lax.dot_general(
-            low, v, over_rows, preferred_element_type=full
+        attn_t = lax.dot_general(v, low, over_rows, preferred_element_type=full)
+        grad_q_t = lax.dot_general(k, score_low, over_rows, preferred_element_type=full) * scale
+        for_queries.append((attn_t.astype(jnp.bfloat16), grad_q_t.astype(jnp.bfloat16)))
+        grad_ref[1, :, part] = (
+            jnp.dot(score_low, q, preferred_element_type=full) * scale
         ).astype(jnp.bfloat16)
-        grad_ref[0, :, part] = (
-            lax.dot_general(score_low, k, over_rows, preferred_element_type=full) * scale
-        ).astype(jnp.bfloat16)
-        grad_ref[1, :, part] = (jnp.dot(score_low, q, preferred_element_type=full) * scale).astype(
-            jnp.bfloat16
-        )
         grad_ref[2, :, part] = jnp.dot(low, g, preferred_element_type=full).astype(jnp.bfloat16)
+    attn_ref[...] = jnp.concatenate([attn for attn, _ in for_queries], 0).T
+    grad_ref[0] = jnp.concatenate([grad for _, grad in for_queries], 0).T
 
 
 def attend(qkv, dout, mask):
@@ -117,11 +118,11 @@
             bytes_accessed=8 * rows * width * 2,
             transcendentals=work * ROWS * ROWS,
         ),
-        compiler_params=pltpu.CompilerParams(vmem_limit_bytes=32 * 2**20),
+        compiler_params=pltpu.CompilerParams(vmem_limit_bytes=58 * 2**20),
     )(qkv, qkv, qkv, dout, mask)
 
 
-LIMIT = pltpu.CompilerParams(vmem_limit_bytes=40 * 2**20)
+LIMIT = pltpu.CompilerParams(vmem_limit_bytes=58 * 2**20)
 
 
 def cost(flops, bytes_accessed):
@@ -298,6 +299,13 @@
         columns = jnp.where(first, outer, outer & 2)
         low_y = jnp.where(first, zero, outer & 1)
         return (columns, low_y), (columns + core, low_y + (1 - core))
+
+    def unit_of(outer, inner):
+        return (
+            jnp.where(first, outer, (outer & 2) + (inner >> 1)),
+            jnp.where(first, inner >> 1, inner & 1),
+            jnp.where(first, inner, outer) & 1,
+        )
 
     inner_at, outer_at = jnp.where(first, y, x), jnp.where(first, x, y)
 
@@ -359,27 +367,23 @@
     )
     share = lax.dynamic_slice(mine, (zero, block_of(x, y) * 256), (own_rows, 256))
     lined = trade_z(jnp.broadcast_to(share, (8, own_rows, 256)))
-    quarters = jnp.zeros((4, 8, own_rows, 256), low)
-    for d in range(4):
-        piece = crossed(lined, d, 1) if d else lined
-        quarters = lax.dynamic_update_slice(
-            quarters, piece[None], (quarter_of((inner_at - d) & 3), zero, zero, zero)
-        )
+    quarters = jnp.stack([lined] + [crossed(lined, d, 1) for d in range(1, 4)])
     weights = jnp.zeros((4, 2, 8, 2, own_rows, 256), low)
     for d in range(4):
         piece = crossed(quarters, d, 0) if d else quarters
         if d == 1:
             piece = follow(piece, (hidden_t, mask, grads_own_first))
-        for i, (columns, low_y) in enumerate(pairs_of((outer_at - d) & 3)):
+        for e in range(4):
+            columns, side, low_y = unit_of((outer_at - d) & 3, (inner_at - e) & 3)
             weights = lax.dynamic_update_slice(
                 weights,
-                piece[2 * i : 2 * i + 2].reshape(1, 2, 8, 1, own_rows, 256),
-                (columns, zero, zero, low_y, zero, zero),
+                piece[e].reshape(1, 1, 8, 1, own_rows, 256),
+                (columns, side, zero, low_y, zero, zero),
             )
     weights = weights.reshape(8, width, 256)
-    proj = weights[6:]
-    kept = lax.dynamic_slice(proj, (zero, core * half, zero), (2, half, 256))
-    got = swap(lax.dynamic_slice(proj, (zero, (1 - core) * half, zero), (2, half, 256)))
+    six = jnp.uint32(6)
+    kept = lax.dynamic_slice(weights, (six, core * half, zero), (2, half, 256))
+    got = swap(lax.dynamic_slice(weights, (six, (1 - core) * half, zero), (2, half, 256)))
 
     biases = qkv_bias.reshape(3, 2, half)
     biases = jnp.where(first, biases[:, 0], biases[:, 1]).reshape(1, -1)
@@ -412,7 +416,7 @@
         sums = sums + crossed(pieces[d], d, 0).astype(full)
     sums = sums.astype(low)
 
-    partial, gain_term, bias_term = find_hidden_grad(grad_qkv, weights, normed, pieces[1:])
+    partial, gain_term, bias_term = find_hidden_grad(grad_qkv, weights, normed, [piece[0, 0, :16, :128] for piece in pieces[1:]])
     bias_term = bias_term.reshape(3, 1, half)
     nothing = jnp.zeros_like(bias_term)
     bias_term = jnp.where(
@@ -441,16 +445,11 @@
         total = total + arrived[:-32].astype(full)
         small = small + joined(arrived)
     sums = total.astype(low).reshape(8, own_rows, 256)
-    repeated = jnp.broadcast_to(split(small), (8, 32, 256))
+    repeated = jnp.broadcast_to(small.astype(low), (8, 16, 256))
     arrived = trade_z(jnp.concatenate([sums, repeated], 1))
-    small = jnp.sum(arrived[:, own_rows:].astype(full), 0)
-    small = small[:16] + small[16:]
-    final = with_small(
-        jnp.sum(arrived[:, :own_rows].astype(full), 0).astype(low), split(small)
-    )
-    arrived = trade_space(jnp.broadcast_to(final, (8, own_rows + 32, 256)))
+    final = jnp.sum(arrived.astype(full), 0).astype(low)
+    arrived = trade_space(jnp.broadcast_to(final, (8, own_rows + 16, 256)))
     small = jnp.sum(arrived[:4, own_rows:].astype(full), 0)
-    small = small[:16] + small[16:]
     rows = arrived[:, :own_rows]
     rows = jnp.where(
         first, rows.reshape(2, 4, own_rows, 256).swapaxes(0, 1).reshape(rows.shape), rows

time: 208 us -> 218 us (1.048)
  Pallas kernels: 32.4 us -> 46.2 us
  waiting for transfers between devices: 49.7 us -> 36.8 us
  other arithmetic: 29.7 us -> 33.7 us
  starting transfers between devices: 47.5 us -> 50.1 us
    ppermute x12, waiting for transfers between devices: 26 us -> 17.3 us  [crossed(): return lax.ppermute(block, BOTH, route(where))]
    unnamed x61 -> x53, local copies, waits for them, and re-layouts: 7.59 us -> 1.69 us
    all_to_all x2, waiting for transfers between devices: 15.9 us -> 12 us  [trade_z(): lax.all_to_all(blocks, 'batch', 0, 0, tiled=True, axis_index_groups=groups)]
    pallas_call x1, Pallas kernels: 3.42 us -> 7.05 us  [project(): pl.pallas_call(project_kernel, grid=(6,), in_specs=[pl.BlockSpec((rows, w...]
    pallas_call x1, Pallas kernels: 3.77 us -> 7.2 us  [find_terms(): pl.pallas_call(terms_kernel, grid=(6,), in_specs=[pl.BlockSpec((width, ro...]
    pallas_call x1, Pallas kernels: 7.08 us -> 9.98 us  [find_hidden_grad(): pl.pallas_call(hidden_grad_kernel, grid=(6,), in_specs=[pl.BlockSpec((1,...]
    ppermute x12, starting transfers between devices: 20.5 us -> 23.3 us  [crossed(): return lax.ppermute(block, BOTH, route(where))]
    another operation x1 -> x2, other arithmetic: 0.39 us -> 2.6 us  [the longest x1 2.21 us: per_device(): quarters = jnp.stack([lined] + [crossed(lined, d, 1) for d in range(1, 4)])]
  transfers between devices with their start and end apart: 25 -> 25, of which waited for: 10 -> 9; matrix products, arithmetic and copies ran while one was open for 26% -> 30% of each run, Pallas kernels for 7% -> 11%
where the time goes in v1:
time: 218 us; the launch traced here: 216 us
  starting transfers between devices  50.1 us (23%)
  local copies, waits for them, and re-layouts  47.4 us (22%)
  Pallas kernels  46.2 us (21%)
  waiting for transfers between devices  36.8 us (17%)
  other arithmetic  33.7 us (15%)
    ppermute x12, starting transfers between devices, crossed(): return lax.ppermute(block, BOTH, route(where))  23.3 us
    dynamic_update_slice x16, local copies, waits for them, and re-layouts, per_device(): lax.dynamic_update_slice(weights, piece[e].reshape(1, 1, 8, 1, own_rows,...  21.2 us
    ppermute x12, waiting for transfers between devices, crossed(): return lax.ppermute(block, BOTH, route(where))  17.3 us
    pallas_call x1, Pallas kernels, attend(): pl.pallas_call(attention_kernel, grid=(2, pairs), in_specs=[columns(0), c...  14.9 us
    all_to_all x2, waiting for transfers between devices, trade_z(): lax.all_to_all(blocks, 'batch', 0, 0, tiled=True, axis_index_groups=groups)  12 us
    pallas_call x1, Pallas kernels, find_hidden_grad(): pl.pallas_call(hidden_grad_kernel, grid=(6,), in_specs=[pl.BlockSpec((1,...  9.98 us
    all_to_all x2, starting transfers between devices, trade_z(): lax.all_to_all(blocks, 'batch', 0, 0, tiled=True, axis_index_groups=groups)  9.88 us
    ppermute x8, starting transfers between devices, swap(): return lax.ppermute(block, BOTH, route(lambda x, y, z, c: (x, y, z, 1 - c)))  8.6 us
  transfers between devices with their start and end apart: 25, of which 9 were waited for; matrix products, arithmetic and copies ran while one was open for 30% of the time, Pallas kernels for 11%

profile of v1, /device:TPU:1, one launch (start us, length us, event | category | flops | bytes accessed | tf_op | source)
XLA Modules:
  0.0 216.0 jit_solution(2546562395821106474)
XLA Ops:
  3.8 3.3 %collective-permute-start = (bf16[1,7,7,7,1024]{4,3,2,1,0:T(8,128)(2,1)S(1)}, bf16[1,7,7,7,1024]{4,3,2,1,0:T(8,128)(2,1)}, u32[]{:S(2)}, u32[]{:S(2)}) collective-permute-start(bf16[1,7,7,7,1024]{4,3,2,1,0:T(8,128)(2,1)S(1)} %pad_maximum_fusion.11), channel_id=1, source_target_pairs={{16,0},{32,16},{48,32},{64,48},{80,64},{96,80},{112,96},{128,112},... | collective-permute-start | bytes 2107400 | tf_op jit(solution)/shard_map/ppermute | solution.py:313
  9.0 6.5 %all-to-all-start = ((bf16[8,64,256]{2,1,0:T(8,128)(2,1)}), bf16[8,64,256]{2,1,0:T(8,128)(2,1)S(1)}, u32[]{:S(2)}, u32[]{:S(2)}) async-start(bf16[8,64,256]{2,1,0:T(8,128)(2,1)} %broadcast_in_dim.62), calls=%async_computation | async-start | bytes 524288 | tf_op jit(solution)/shard_map/all_to_all | solution.py:51
  18.0 6.7 %all-to-all-done = bf16[8,64,256]{2,1,0:T(8,128)(2,1)S(1)} async-done(((bf16[8,64,256]{2,1,0:T(8,128)(2,1)}), bf16[8,64,256]{2,1,0:T(8,128)(2,1)S(1)}, u32[]{:S(2)}, u32[]{:S(2)}) %all-to-all-start) | async-done | bytes 262176 | tf_op jit(solution)/shard_map/all_to_all | solution.py:51
  24.7 4.2 %collective-permute-start.2 = (bf16[8,64,256]{2,1,0:T(8,128)(2,1)S(1)}, bf16[8,64,256]{2,1,0:T(8,128)(2,1)}, u32[]{:S(2)}, u32[]{:S(2)}) collective-permute-start(bf16[8,64,256]{2,1,0:T(8,128)(2,1)S(1)} %all-to-all-done), channel_id=1, source_target_pairs={{0,1},{16,48},{2,3},{18,50},{4,5},{20,52},{6,7},{22,54},{8,9},{24,... | collective-permute-start | bytes 786440 | tf_op jit(solution)/shard_map/ppermute | solution.py:46
  29.0 1.9 collective-permute-start.3
  38.0 1.9 collective-permute-start.1
  42.7 1.8 fusion.64
  45.6 2.2 %pad_maximum_fusion.3 = bf16[4,8,64,256]{3,2,1,0:T(8,128)(2,1)} fusion(bf16[1,8,64,256]{3,2,1,0:T(8,128)(2,1)} %bitcast.13, bf16[1,8,64,256]{3,2,1,0:T(8,128)(2,1)} %bitcast.12, bf16[1,8,64,256]{3,2,1,0:T(8,128)(2,1)} %bitcast.11, bf16[1,8,64,256]{3,2,1,0:T(8,128)(2,1)S(1)} %bitcast.235), kind=kLoop, calls=%fused_computation.28 | loop fusion | flops 1572864 | bytes 2097152 | tf_op jit(solution)/shard_map/stack | solution.py:370
  50.4 2.0 collective-permute-start.8
  58.2 2.6 %multiply_convert_fusion = (bf16[704,1024]{1,0:T(8,128)(2,1)}, f32[704,1024]{1,0:T(8,128)}) fusion(f32[1024]{0:T(1024)S(1)} %copy-done.15, f32[704]{0:T(1024)S(1)} %add_rsqrt_fusion, f32[704]{0:T(1024)S(1)} %broadcast_multiply_fusion, bf16[352,1024]{1,0:T(8,128)(2,1)S(1)} %collective-permute-done.1, bf16[352,1024]{1,0:T(8,128)(2,1)S(1)} %pad.36), kind=kLoop, calls=%fused_computation.5 | loop fusion | flops 5767168 | bytes 5776896 | tf_op jit(solution)/shard_map/convert_element_type | solution.py:340
  60.8 2.6 %copy.187.refs_1_.left_ref = bf16[1024,704]{1,0:T(8,128)(2,1)} copy(bf16[1024,704]{0,1:T(8,128)(2,1)} %bitcast.234) | data formatting | bytes 2883584 | tf_op jit(solution)/shard_map/transpose | solution.py:341
  84.8 2.1 constant_dynamic-slice_fusion.4
  88.8 7.1 %shard_map.111.q_ref.k_ref.v_ref = bf16[704,1536]{1,0:T(8,128)(2,1)} custom-call(bf16[704,1024]{1,0:T(8,128)(2,1)} %get-tuple-element.31.hidden_ref, bf16[8,1024,256]{2,1,0:T(8,128)(2,1)} %bitcast.231, f32[1,1536]{1,0:T(1,128)} %bitcast.246), custom_call_target="tpu_custom_call" | custom-call | flops 2214592512 | bytes 8388608 | tf_op jit(solution)/shard_map/pallas_call | solution.py:151
  96.6 3.4 %shard_map.112.g_ref = bf16[704,512]{1,0:T(8,128)(2,1)} custom-call(bf16[704,1024]{1,0:T(8,128)(2,1)} %fusion.3.refs_3_.grad_ref.right_ref, bf16[2,512,256]{2,1,0:T(8,128)(2,1)} %get-tuple-element.29.kept_ref, bf16[2,512,256]{2,1,0:T(8,128)(2,1)} %copy-done.8), custom_call_target="tpu_custom_call" | custom-call | flops 738197504 | bytes 4194304 | tf_op jit(solution)/shard_map/pallas_call | solution.py:180
  100.1 14.9 %shard_map.113 = (bf16[704,512]{1,0:T(8,128)(2,1)}, bf16[3,704,512]{2,1,0:T(8,128)(2,1)}) custom-call(bf16[704,1536]{1,0:T(8,128)(2,1)} %shard_map.111.q_ref.k_ref.v_ref, bf16[704,1536]{1,0:T(8,128)(2,1)} %shard_map.111.q_ref.k_ref.v_ref, bf16[704,1536]{1,0:T(8,128)(2,1)} %shard_map.111.q_ref.k_ref.v_ref, bf16[704,512]{1,0:T(8,128)(2,1)} %shard_map.112.g_ref, ...), custom_call_target="tpu_custom_call" | custom-call | flops 7105150976 | bytes 5767168 | tf_op jit(solution)/shard_map/pallas_call | solution.py:101
  115.0 7.2 %shard_map.114.terms_ref = bf16[8,1024,256]{2,1,0:T(8,128)(2,1)} custom-call(bf16[1024,704]{1,0:T(8,128)(2,1)} %copy.187.refs_1_.left_ref, bf16[3,704,512]{2,1,0:T(8,128)(2,1)} %get-tuple-element.10.right_ref.grad_ref), custom_call_target="tpu_custom_call" | custom-call | flops 2214592512 | bytes 8388608 | tf_op jit(solution)/shard_map/pallas_call | solution.py:196
  123.8 3.6 %shard_map.115 = bf16[8,1024,256]{2,1,0:T(8,128)(2,1)} custom-call(bf16[704,1024]{1,0:T(8,128)(2,1)} %maximum_select_fusion.left_ref, bf16[704,1024]{1,0:T(8,128)(2,1)} %fusion.3.refs_3_.grad_ref.right_ref, bf16[8,1024,256]{2,1,0:T(8,128)(2,1)} %shard_map.114.terms_ref), custom_call_target="tpu_custom_call", output_to_operand_aliasing={{}: (2, {})} | custom-call | flops 738197504 | bytes 4194304 | tf_op jit(solution)/shard_map/pallas_call | solution.py:218
  127.4 2.7 %dynamic-slice_bitcast_fusion.4 = (bf16[2,8,64,256]{3,2,1,0:T(8,128)(2,1)S(1)}, bf16[2,8,64,256]{3,2,1,0:T(8,128)(2,1)S(1)}, bf16[2,8,64,256]{3,2,1,0:T(8,128)(2...) fusion(bf16[4,2,8,2,64,256]{5,4,3,2,1,0:T(8,128)(2,1)} %bitcast, ...), kind=kLoop, calls=%fused_computation.68 | loop fusion | bytes 8388672 | tf_op jit(solution)/shard_map/reshape | solution.py:407
  132.4 7.1 %collective-permute-start.15 = (bf16[4,8,64,256]{3,2,1,0:T(8,128)(2,1)}, bf16[4,8,64,256]{3,2,1,0:T(8,128)(2,1)S(1)}, u32[]{:S(2)}, u32[]{:S(2)}) collective-permute-start(bf16[4,8,64,256]{3,2,1,0:T(8,128)(2,1)} %pad_maximum_fusion.6), channel_id=1, source_target_pairs={{0,96},{16,145},{2,98},{18,147},{4,100},{20,149},{6,102},{22,151},... | collective-permute-start | bytes 3145736 | tf_op jit(solution)/shard_map/ppermute | solution.py:46
  144.5 10.0 %shard_map.116 = (f32[704,1024]{1,0:T(8,128)}, f32[1,1024]{1,0:T(1,128)}, f32[6,1,256]{2,1,0:T(1,128)}) custom-call(bf16[3,704,512]{2,1,0:T(8,128)(2,1)} %get-tuple-element.10.right_ref.grad_ref, bf16[8,1024,256]{2,1,0:T(8,128)(2,1)} %bitcast.232, f32[704,1024]{1,0:T(8,128)} %get-tuple-element.32.normed_ref, bf16[16,128]{1,0:T(8,128)(2,1)} %slice_bitcast_fusion.32.rest_0_, ...), custom_call_target="tpu_custom_call" | custom-call | flops 2214592512 | bytes 14680064 | tf_op jit(solution)/shard_map/pallas_call | solution.py:258
  156.0 2.6 %slice.349 = f32[352,1024]{1,0:T(8,128)} slice(f32[704,1024]{1,0:T(8,128)} %get-tuple-element.12), slice={[352:704], [0:1024]} | slice | bytes 2883584 | tf_op jit(solution)/shard_map/slice | solution.py:465
  159.1 3.6 %collective-permute-done.15 = bf16[4,8,64,256]{3,2,1,0:T(8,128)(2,1)S(1)} collective-permute-done((bf16[4,8,64,256]{3,2,1,0:T(8,128)(2,1)}, bf16[4,8,64,256]{3,2,1,0:T(8,128)(2,1)S(1)}, u32[]{:S(2)}, u32[]{:S(2)}) %collective-permute-start.15) | collective-permute-done | bytes 1048608 | tf_op jit(solution)/shard_map/ppermute | solution.py:46
  162.8 4.8 %collective-permute-done.13 = bf16[4,8,64,256]{3,2,1,0:T(8,128)(2,1)} collective-permute-done((bf16[4,8,64,256]{3,2,1,0:T(8,128)(2,1)}, bf16[4,8,64,256]{3,2,1,0:T(8,128)(2,1)}, u32[]{:S(2)}, u32[]{:S(2)}) %collective-permute-start.13) | collective-permute-done | bytes 1048608 | tf_op jit(solution)/shard_map/ppermute | solution.py:46
  167.6 1.9 add_convert_fusion
  171.2 4.2 %collective-permute-done.19 = bf16[544,256]{1,0:T(8,128)(2,1)S(1)} collective-permute-done((bf16[544,256]{1,0:T(8,128)(2,1)S(1)}, bf16[544,256]{1,0:T(8,128)(2,1)S(1)}, u32[]{:S(2)}, u32[]{:S(2)}) %collective-permute-start.19) | collective-permute-done | bytes 278560 | tf_op jit(solution)/shard_map/ppermute | solution.py:46
  177.1 2.9 %collective-permute-done.17 = bf16[544,256]{1,0:T(8,128)(2,1)S(1)} collective-permute-done((bf16[544,256]{1,0:T(8,128)(2,1)S(1)}, bf16[544,256]{1,0:T(8,128)(2,1)S(1)}, u32[]{:S(2)}, u32[]{:S(2)}) %collective-permute-start.17) | collective-permute-done | bytes 278560 | tf_op jit(solution)/shard_map/ppermute | solution.py:46
  181.0 3.4 %all-to-all-start.1 = ((bf16[8,80,256]{2,1,0:T(8,128)(2,1)}), bf16[8,80,256]{2,1,0:T(8,128)(2,1)S(1)}, u32[]{:S(2)}, u32[]{:S(2)}) async-start(bf16[8,80,256]{2,1,0:T(8,128)(2,1)} %pad_maximum_fusion.21), calls=%async_computation.1 | async-start | bytes 655360 | tf_op jit(solution)/shard_map/all_to_all | solution.py:51
  184.5 2.4 %fusion.61 = (f32[352]{0:T(512)S(1)}, f32[352]{0:T(512)S(1)}, f32[352,1024]{1,0:T(8,128)S(1)}, f32[352,1024]{1,0:T(8,128)S(1)}) fusion(f32[704,1024]{1,0:T(8,128)S(1)} %copy-done.1, f32[1024]{0:T(1024)S(1)} %copy-done.15, f32[352,1024]{1,0:T(8,128)} %collective-permute-done.11, f32[704,1024]{1,0:T(8,128)} %get-tuple-element.12), kind=kLoop, calls=%fused_computation.206 | loop fusion | flops 1801536 | bytes 7215872 | tf_op jit(solution)/shard_map/reduce_sum | solution.py:470
  189.0 5.3 %all-to-all-done.1 = bf16[8,80,256]{2,1,0:T(8,128)(2,1)S(1)} async-done(((bf16[8,80,256]{2,1,0:T(8,128)(2,1)}), bf16[8,80,256]{2,1,0:T(8,128)(2,1)S(1)}, u32[]{:S(2)}, u32[]{:S(2)}) %all-to-all-start.1) | async-done | bytes 327712 | tf_op jit(solution)/shard_map/all_to_all | solution.py:51
  195.1 4.0 %all-to-all-start.2 = ((bf16[8,80,256]{2,1,0:T(8,128)(2,1)}), bf16[8,80,256]{2,1,0:T(8,128)(2,1)S(1)}, u32[]{:S(2)}, u32[]{:S(2)}) async-start(bf16[8,80,256]{2,1,0:T(8,128)(2,1)} %broadcast_in_dim.70), calls=%async_computation.2 | async-start | bytes 655360 | tf_op jit(solution)/shard_map/all_to_all | solution.py:56
  200.3 6.8 %all-to-all-done.2 = bf16[8,80,256]{2,1,0:T(8,128)(2,1)S(1)} async-done(((bf16[8,80,256]{2,1,0:T(8,128)(2,1)}), bf16[8,80,256]{2,1,0:T(8,128)(2,1)S(1)}, u32[]{:S(2)}, u32[]{:S(2)}) %all-to-all-start.2) | async-done | bytes 327712 | tf_op jit(solution)/shard_map/all_to_all | solution.py:56
  207.2 4.8 %collective-permute-start.21 = (f32[16,256]{1,0:T(8,128)S(1)}, f32[16,256]{1,0:T(8,128)S(1)}, u32[]{:S(2)}, u32[]{:S(2)}) collective-permute-start(f32[16,256]{1,0:T(8,128)S(1)} %convert_reduce_fusion.1), channel_id=1, source_target_pairs={{0,16},{16,0},{2,18},{18,2},{4,20},{20,4},{6,22},{22,6},{8,24},{24... | collective-permute-start | bytes 49160 | tf_op jit(solution)/shard_map/ppermute | solution.py:37
  (215 shorter events, 73.6 us)
Async XLA Ops:
  3.8 11.7 %copy-start.5 = (bf16[1,7,7,7,1024]{4,3,2,1,0:T(8,128)(2,1)S(1)}, bf16[1,7,7,7,1024]{4,3,2,1,0:T(8,128)(2,1)}, u32[]{:S(2)}) copy-start(bf16[1,7,7,7,1024]{4,3,2,1,0:T(8,128)(2,1)} %param.7) | copy-start | bytes 2107396
  3.8 29.4 %collective-permute-start = (bf16[1,7,7,7,1024]{4,3,2,1,0:T(8,128)(2,1)S(1)}, bf16[1,7,7,7,1024]{4,3,2,1,0:T(8,128)(2,1)}, u32[]{:S(2)}, u32[]{:S(2)}) collective-permute-start(bf16[1,7,7,7,1024]{4,3,2,1,0:T(8,128)(2,1)S(1)} %pad_maximum_fusion.11), channel_id=1, source_target_pairs={{16,0},{32,16},{48,32},{64,48},{80,64},{96,80},{112,96},{128,112},... | collective-permute-start | bytes 2107400 | tf_op jit(solution)/shard_map/ppermute | solution.py:313
  7.4 8.1 %copy-start.6 = (bf16[1,7,7,7,1024]{4,3,2,1,0:T(8,128)(2,1)S(1)}, bf16[1,7,7,7,1024]{4,3,2,1,0:T(8,128)(2,1)}, u32[]{:S(2)}) copy-start(bf16[1,7,7,7,1024]{4,3,2,1,0:T(8,128)(2,1)} %param.8) | copy-start | bytes 2107396
  7.4 8.2 %copy-start.11 = (s32[7,7,7]{2,1,0:T(8,128)S(1)}, s32[7,7,7]{2,1,0:T(8,128)}, u32[]{:S(2)}) copy-start(s32[7,7,7]{2,1,0:T(8,128)} %param.9) | copy-start | bytes 4120
  9.0 15.8 %all-to-all-start = ((bf16[8,64,256]{2,1,0:T(8,128)(2,1)}), bf16[8,64,256]{2,1,0:T(8,128)(2,1)S(1)}, u32[]{:S(2)}, u32[]{:S(2)}) async-start(bf16[8,64,256]{2,1,0:T(8,128)(2,1)} %broadcast_in_dim.62), calls=%async_computation | async-start | bytes 524288 | tf_op jit(solution)/shard_map/all_to_all | solution.py:51
  24.7 20.8 %collective-permute-start.2 = (bf16[8,64,256]{2,1,0:T(8,128)(2,1)S(1)}, bf16[8,64,256]{2,1,0:T(8,128)(2,1)}, u32[]{:S(2)}, u32[]{:S(2)}) collective-permute-start(bf16[8,64,256]{2,1,0:T(8,128)(2,1)S(1)} %all-to-all-done), channel_id=1, source_target_pairs={{0,1},{16,48},{2,3},{18,50},{4,5},{20,52},{6,7},{22,54},{8,9},{24,... | collective-permute-start | bytes 786440 | tf_op jit(solution)/shard_map/ppermute | solution.py:46
  29.0 16.6 %collective-permute-start.3 = (bf16[8,64,256]{2,1,0:T(8,128)(2,1)S(1)}, bf16[8,64,256]{2,1,0:T(8,128)(2,1)}, u32[]{:S(2)}, u32[]{:S(2)}) collective-permute-start(bf16[8,64,256]{2,1,0:T(8,128)(2,1)S(1)} %all-to-all-done), channel_id=1, source_target_pairs={{0,128},{16,80},{2,130},{18,82},{4,132},{20,84},{6,134},{22,86},{8... | collective-permute-start | bytes 786440 | tf_op jit(solution)/shard_map/ppermute | solution.py:46
  30.9 14.7 %collective-permute-start.4 = (bf16[8,64,256]{2,1,0:T(8,128)(2,1)S(1)}, bf16[8,64,256]{2,1,0:T(8,128)(2,1)}, u32[]{:S(2)}, u32[]{:S(2)}) collective-permute-start(bf16[8,64,256]{2,1,0:T(8,128)(2,1)S(1)} %all-to-all-done), channel_id=1, source_target_pairs={{0,129},{16,112},{2,131},{18,114},{4,133},{20,116},{6,135},{22,118... | collective-permute-start | bytes 786440 | tf_op jit(solution)/shard_map/ppermute | solution.py:46
  38.0 19.4 %collective-permute-start.1 = (bf16[352,1024]{1,0:T(8,128)(2,1)S(1)}, bf16[352,1024]{1,0:T(8,128)(2,1)S(1)}, u32[]{:S(2)}, u32[]{:S(2)}) collective-permute-start(bf16[352,1024]{1,0:T(8,128)(2,1)S(1)} %pad.36), channel_id=1, source_target_pairs={{0,16},{16,0},{2,18},{18,2},{4,20},{20,4},{6,22},{22,6},{8,24},{24... | collective-permute-start | bytes 2162696 | tf_op jit(solution)/shard_map/ppermute | solution.py:37
  44.4 19.0 %collective-permute-start.6 = (bf16[352,1024]{1,0:T(8,128)(2,1)}, bf16[352,1024]{1,0:T(8,128)(2,1)}, u32[]{:S(2)}, u32[]{:S(2)}) collective-permute-start(bf16[352,1024]{1,0:T(8,128)(2,1)} %get-tuple-element.44), channel_id=1, source_target_pairs={{0,16},{16,0},{2,18},{18,2},{4,20},{20,4},{6,22},{22,6},{8,24},{24... | collective-permute-start | bytes 2162696 | tf_op jit(solution)/shard_map/ppermute | solution.py:37
  47.8 10.4 %copy-start.15 = (f32[1024]{0:T(1024)S(1)}, f32[1024]{0:T(1024)}, u32[]{:S(2)}) copy-start(f32[1024]{0:T(1024)} %param.13) | copy-start | bytes 12292
  47.8 20.8 %collective-permute-start.5 = (bf16[4,8,64,256]{3,2,1,0:T(8,128)(2,1)}, bf16[4,8,64,256]{3,2,1,0:T(8,128)(2,1)}, u32[]{:S(2)}, u32[]{:S(2)}) collective-permute-start(bf16[4,8,64,256]{3,2,1,0:T(8,128)(2,1)} %pad_maximum_fusion.3), channel_id=1, source_target_pairs={{0,32},{16,17},{2,34},{18,19},{4,36},{20,21},{6,38},{22,23},{8,40}... | collective-permute-start | bytes 3145736 | tf_op jit(solution)/shard_map/ppermute | solution.py:46
  48.7 26.5 %collective-permute-start.7 = (bf16[4,8,64,256]{3,2,1,0:T(8,128)(2,1)}, bf16[4,8,64,256]{3,2,1,0:T(8,128)(2,1)}, u32[]{:S(2)}, u32[]{:S(2)}) collective-permute-start(bf16[4,8,64,256]{3,2,1,0:T(8,128)(2,1)} %pad_maximum_fusion.3), channel_id=1, source_target_pairs={{0,64},{16,144},{2,66},{18,146},{4,68},{20,148},{6,70},{22,150},{8... | collective-permute-start | bytes 3145736 | tf_op jit(solution)/shard_map/ppermute | solution.py:46
  50.4 31.5 %collective-permute-start.8 = (bf16[4,8,64,256]{3,2,1,0:T(8,128)(2,1)}, bf16[4,8,64,256]{3,2,1,0:T(8,128)(2,1)S(1)}, u32[]{:S(2)}, u32[]{:S(2)}) collective-permute-start(bf16[4,8,64,256]{3,2,1,0:T(8,128)(2,1)} %pad_maximum_fusion.3), channel_id=1, source_target_pairs={{0,96},{16,145},{2,98},{18,147},{4,100},{20,149},{6,102},{22,151},... | collective-permute-start | bytes 3145736 | tf_op jit(solution)/shard_map/ppermute | solution.py:46
  58.2 113.0 %copy-start.12 = (f32[704]{0:T(1024)}, f32[704]{0:T(1024)S(1)}, u32[]{:S(2)}) copy-start(f32[704]{0:T(1024)S(1)} %add_rsqrt_fusion) | copy-start | bytes 8452
  86.8 9.0 %collective-permute-start.9 = (bf16[2,512,256]{2,1,0:T(8,128)(2,1)S(1)}, bf16[2,512,256]{2,1,0:T(8,128)(2,1)S(1)}, u32[]{:S(2)}, u32[]{:S(2)}) collective-permute-start(bf16[2,512,256]{2,1,0:T(8,128)(2,1)S(1)} %get-tuple-element.28), channel_id=1, source_target_pairs={{0,16},{16,0},{2,18},{18,2},{4,20},{20,4},{6,22},{22,6},{8,24},{24... | collective-permute-start | bytes 1572872 | tf_op jit(solution)/shard_map/ppermute | solution.py:37
  115.0 7.2 %collective-permute-start.10 = (bf16[704,512]{1,0:T(8,128)(2,1)}, bf16[704,512]{1,0:T(8,128)(2,1)S(1)}, u32[]{:S(2)}, u32[]{:S(2)}) collective-permute-start(bf16[704,512]{1,0:T(8,128)(2,1)} %get-tuple-element.11), channel_id=1, source_target_pairs={{0,16},{16,0},{2,18},{18,2},{4,20},{20,4},{6,22},{22,6},{8,24},{24... | collective-permute-start | bytes 2162696 | tf_op jit(solution)/shard_map/ppermute | solution.py:37
  115.0 7.3 %copy-start.7 = (bf16[704,512]{1,0:T(8,128)(2,1)S(1)}, bf16[704,512]{1,0:T(8,128)(2,1)}, u32[]{:S(2)}) copy-start(bf16[704,512]{1,0:T(8,128)(2,1)} %get-tuple-element.11) | copy-start | bytes 2162692
  132.4 30.4 %collective-permute-start.15 = (bf16[4,8,64,256]{3,2,1,0:T(8,128)(2,1)}, bf16[4,8,64,256]{3,2,1,0:T(8,128)(2,1)S(1)}, u32[]{:S(2)}, u32[]{:S(2)}) collective-permute-start(bf16[4,8,64,256]{3,2,1,0:T(8,128)(2,1)} %pad_maximum_fusion.6), channel_id=1, source_target_pairs={{0,96},{16,145},{2,98},{18,147},{4,100},{20,149},{6,102},{22,151},... | collective-permute-start | bytes 3145736 | tf_op jit(solution)/shard_map/ppermute | solution.py:46
  140.6 22.2 %collective-permute-start.14 = (bf16[4,8,64,256]{3,2,1,0:T(8,128)(2,1)}, bf16[4,8,64,256]{3,2,1,0:T(8,128)(2,1)S(1)}, u32[]{:S(2)}, u32[]{:S(2)}) collective-permute-start(bf16[4,8,64,256]{3,2,1,0:T(8,128)(2,1)} %pad_maximum_fusion.5), channel_id=1, source_target_pairs={{0,64},{16,144},{2,66},{18,146},{4,68},{20,148},{6,70},{22,150},{8... | collective-permute-start | bytes 3145736 | tf_op jit(solution)/shard_map/ppermute | solution.py:46
  143.0 24.5 %collective-permute-start.13 = (bf16[4,8,64,256]{3,2,1,0:T(8,128)(2,1)}, bf16[4,8,64,256]{3,2,1,0:T(8,128)(2,1)}, u32[]{:S(2)}, u32[]{:S(2)}) collective-permute-start(bf16[4,8,64,256]{3,2,1,0:T(8,128)(2,1)} %pad_maximum_fusion.4), channel_id=1, source_target_pairs={{0,32},{16,17},{2,34},{18,19},{4,36},{20,21},{6,38},{22,23},{8,40}... | collective-permute-start | bytes 3145736 | tf_op jit(solution)/shard_map/ppermute | solution.py:46
  155.9 3.2 %collective-permute-start.16 = (f32[16,256]{1,0:T(8,128)S(1)}, f32[16,256]{1,0:T(8,128)S(1)}, u32[]{:S(2)}, u32[]{:S(2)}) collective-permute-start(f32[16,256]{1,0:T(8,128)S(1)} %reshape.479), channel_id=1, source_target_pairs={{0,16},{16,0},{2,18},{18,2},{4,20},{20,4},{6,22},{22,6},{8,24},{24... | collective-permute-start | bytes 49160 | tf_op jit(solution)/shard_map/ppermute | solution.py:37
  158.6 25.8 %collective-permute-start.11 = (f32[352,1024]{1,0:T(8,128)}, f32[352,1024]{1,0:T(8,128)}, u32[]{:S(2)}, u32[]{:S(2)}) collective-permute-start(f32[352,1024]{1,0:T(8,128)} %slice.349), channel_id=1, source_target_pairs={{0,16},{16,0},{2,18},{18,2},{4,20},{20,4},{6,22},{22,6},{8,24},{24... | collective-permute-start | bytes 4325384 | tf_op jit(solution)/shard_map/ppermute | solution.py:37
  169.6 14.9 %copy-start.1 = (f32[704,1024]{1,0:T(8,128)S(1)}, f32[704,1024]{1,0:T(8,128)}, u32[]{:S(2)}) copy-start(f32[704,1024]{1,0:T(8,128)} %get-tuple-element.32.normed_ref) | copy-start | bytes 8650756
  169.7 5.8 %collective-permute-start.19 = (bf16[544,256]{1,0:T(8,128)(2,1)S(1)}, bf16[544,256]{1,0:T(8,128)(2,1)S(1)}, u32[]{:S(2)}, u32[]{:S(2)}) collective-permute-start(bf16[544,256]{1,0:T(8,128)(2,1)S(1)} %get-tuple-element.56), channel_id=1, source_target_pairs={{0,129},{16,112},{2,131},{18,114},{4,133},{20,116},{6,135},{22,118... | collective-permute-start | bytes 835592 | tf_op jit(solution)/shard_map/ppermute | solution.py:46
  169.8 7.3 %collective-permute-start.18 = (bf16[544,256]{1,0:T(8,128)(2,1)S(1)}, bf16[544,256]{1,0:T(8,128)(2,1)S(1)}, u32[]{:S(2)}, u32[]{:S(2)}) collective-permute-start(bf16[544,256]{1,0:T(8,128)(2,1)S(1)} %get-tuple-element.55), channel_id=1, source_target_pairs={{0,128},{16,80},{2,130},{18,82},{4,132},{20,84},{6,134},{22,86},{8... | collective-permute-start | bytes 835592 | tf_op jit(solution)/shard_map/ppermute | solution.py:46
  169.9 10.2 %collective-permute-start.17 = (bf16[544,256]{1,0:T(8,128)(2,1)S(1)}, bf16[544,256]{1,0:T(8,128)(2,1)S(1)}, u32[]{:S(2)}, u32[]{:S(2)}) collective-permute-start(bf16[544,256]{1,0:T(8,128)(2,1)S(1)} %get-tuple-element.54), channel_id=1, source_target_pairs={{0,1},{16,48},{2,3},{18,50},{4,5},{20,52},{6,7},{22,54},{8,9},{24,... | collective-permute-start | bytes 835592 | tf_op jit(solution)/shard_map/ppermute | solution.py:46
  181.0 13.3 %all-to-all-start.1 = ((bf16[8,80,256]{2,1,0:T(8,128)(2,1)}), bf16[8,80,256]{2,1,0:T(8,128)(2,1)S(1)}, u32[]{:S(2)}, u32[]{:S(2)}) async-start(bf16[8,80,256]{2,1,0:T(8,128)(2,1)} %pad_maximum_fusion.21), calls=%async_computation.1 | async-start | bytes 655360 | tf_op jit(solution)/shard_map/all_to_all | solution.py:51
  188.1 11.0 %collective-permute-start.12 = (bf16[1,3,7,7,1024]{4,3,2,1,0:T(8,128)(2,1)S(1)}, bf16[1,3,7,7,1024]{4,3,2,1,0:T(8,128)(2,1)S(1)}, u32[]{:S(2)}, u32[]{:S(2)}) collective-permute-start(bf16[1,3,7,7,1024]{4,3,2,1,0:T(8,128)(2,1)S(1)} %pad_maximum_fusion.20), channel_id=1, source_target_pairs={{0,16},{16,32},{32,48},{48,64},{64,80},{80,96},{96,112},{112,128},... | collective-permute-start | bytes 903176 | tf_op jit(solution)/shard_map/ppermute | solution.py:476
  195.1 12.0 %all-to-all-start.2 = ((bf16[8,80,256]{2,1,0:T(8,128)(2,1)}), bf16[8,80,256]{2,1,0:T(8,128)(2,1)S(1)}, u32[]{:S(2)}, u32[]{:S(2)}) async-start(bf16[8,80,256]{2,1,0:T(8,128)(2,1)} %broadcast_in_dim.70), calls=%async_computation.2 | async-start | bytes 655360 | tf_op jit(solution)/shard_map/all_to_all | solution.py:56
  207.2 5.7 %collective-permute-start.21 = (f32[16,256]{1,0:T(8,128)S(1)}, f32[16,256]{1,0:T(8,128)S(1)}, u32[]{:S(2)}, u32[]{:S(2)}) collective-permute-start(f32[16,256]{1,0:T(8,128)S(1)} %convert_reduce_fusion.1), channel_id=1, source_target_pairs={{0,16},{16,0},{2,18},{18,2},{4,20},{20,4},{6,22},{22,6},{8,24},{24... | collective-permute-start | bytes 49160 | tf_op jit(solution)/shard_map/ppermute | solution.py:37
  212.1 2.0 collective-permute-start.20
  (12 other events, 43.2 us)
